TPU v7x, 256 devices: a whole 4x4x8 slice. The times are simulated.
256 devices in a mesh: gx: 32 (over z, y_hi, core), gy: 8 (over y_lo, x).
Axes of the slice: x: 4, y: 4 (y_hi: 2, y_lo: 2; y = y_hi * 2 + y_lo), z: 8, core: 2. Of those that a mesh axis runs over, the one named last changes fastest.
Arguments:
- features: float32 [32, 8, 24, 64, 128], P('gx', 'gy'), may hold values from -6 to 6
- weights: float32 [27, 64, 64], replicated, may hold values from -0.15625 to 0.15625
- kernel_map: int32 [32, 8, 24, 27], P('gx', 'gy'), may hold values from 0 to 56, as said below
- send_lists: int32 [32, 8, 8, 4], P('gx', 'gy'), may hold values from 0 to 23, as said below
- counts: int32 [32, 8], P('gx', 'gy'), may hold values from 6 to 24, as said below
- cotangent: float32 [32, 8, 24, 64, 128], P('gx', 'gy'), may hold values from -6 to 6
Outputs:
- activations: float32 [32, 8, 24, 64, 128], P('gx', 'gy')
- grad_features: float32 [32, 8, 24, 64, 128], P('gx', 'gy')
- grad_weights: float32 [27, 64, 64], replicated
Inputs may be any that keep to these rules, and one draw needn't show every extreme that they name: `counts`: some device has exactly 24 occupied slots. `send_lists`: every entry names an occupied tile slot of the sending device, below its count. `kernel_map`: entries below 24 name slots of the device itself; offset 13 of slot t is t; entry 24 + r * 4 + h is entry h of halo block r; entry 24 + 32 is the empty tile.
All inputs are finite; a program needn't handle non-finite values.
Results may differ from a plain program's by a relative error of at most 0.0003.
Values sent between devices are 32-bit elements; how exact they have to be, the bound alone decides.
A program may use at most 64 MiB of HBM per device.

v0:
```python
import jax
import jax.numpy as jnp
from jax import lax
from jax.sharding import PartitionSpec as P

OFFSETS = ((-1, -1), (-1, 0), (-1, 1), (0, -1), (0, 1), (1, -1), (1, 0), (1, 1))


def from_behind(value, axis, steps):
    count = lax.axis_size(axis)
    initial, last = (max(0, -steps), min(count, count - steps))
    return lax.ppermute(value, axis, [(source, source + steps) for source in range(initial, last)])


def fetch_block(block, step_x, step_y):
    if step_x != 0:
        block = from_behind(block, "gx", -step_x)
    if step_y != 0:
        block = from_behind(block, "gy", -step_y)
    return block


def give_block(block, step_x, step_y):
    if step_x != 0:
        block = from_behind(block, "gx", step_x)
    if step_y != 0:
        block = from_behind(block, "gy", step_y)
    return block


def halo_in(outgoing):
    position = {offset: slot for slot, offset in enumerate(OFFSETS)}
    arrived = {}
    for offset in OFFSETS:
        arrived[offset] = fetch_block(outgoing[position[offset]], offset[0], offset[1])
    return jnp.stack([arrived[offset] for offset in OFFSETS])


def halo_out(grad_blocks):
    blocks = {offset: grad_blocks[slot] for slot, offset in enumerate(OFFSETS)}
    returned = {}
    for offset in OFFSETS:
        returned[offset] = give_block(blocks[offset], offset[0], offset[1])
    return jnp.stack([returned[offset] for offset in OFFSETS])


def per_device(features, weights, kernel_map, send_lists, counts, cotangent):
    local = features[0, 0]
    kmap = kernel_map[0, 0]
    sends = send_lists[0, 0]
    grad_out = cotangent[0, 0]
    tiles, chan, vox = local.shape
    halo = sends.shape[1]
    live = (lax.iota(jnp.int32, tiles) < counts[0, 0]).astype(jnp.float32)[:, None, None]
    outgoing = local[sends.reshape(-1)].reshape(8, halo, chan, vox)
    received = halo_in(outgoing)
    extended = jnp.concatenate(
        [local, received.reshape(8 * halo, chan, vox), jnp.zeros((1, chan, vox), jnp.float32)],
        axis=0,
    )

    def forward(total, item):
        w_k, column = item
        picked = extended[column]
        return (
            total + jnp.einsum("oc,tcv->tov", w_k, picked, precision=lax.Precision.HIGHEST),
            None,
        )

    pre, _ = lax.scan(forward, jnp.zeros((tiles, chan, vox), jnp.float32), (weights, kmap.T))
    sig = jax.nn.sigmoid(pre)
    act = pre * sig * live
    grad_pre = grad_out * live * sig * (1.0 + pre * (1.0 - sig))

    def backward(acc, item):
        w_k, column = item
        picked = extended[column]
        g_w = jnp.einsum("tov,tcv->oc", grad_pre, picked, precision=lax.Precision.HIGHEST)
        contrib = jnp.einsum("oc,tov->tcv", w_k, grad_pre, precision=lax.Precision.HIGHEST)
        return (acc.at[column].add(contrib), g_w)

    grad_ext, grad_w = lax.scan(backward, jnp.zeros_like(extended), (weights, kmap.T))
    grad_weights = lax.psum(grad_w, ("gx", "gy"))
    back = halo_out(grad_ext[tiles : tiles + 8 * halo].reshape(8, halo, chan, vox))
    grad_x = grad_ext[:tiles].at[sends.reshape(-1)].add(back.reshape(8 * halo, chan, vox))
    return (act[None, None], grad_x[None, None], grad_weights)


def solution(mesh):
    placed = (
        P("gx", "gy", None, None, None),
        P(),
        P("gx", "gy", None, None),
        P("gx", "gy", None, None),
        P("gx", "gy"),
        P("gx", "gy", None, None, None),
    )
    return jax.shard_map(
        per_device,
        mesh=mesh,
        in_specs=placed,
        out_specs=(P("gx", "gy", None, None, None), P("gx", "gy", None, None, None), P()),
        check_vma=False,
    )
```

profile of v0, /device:TPU:1, one launch (start us, length us, event | category | flops | bytes accessed | tf_op | source)
XLA Modules:
  0.0 649.7 jit_solution(13021435946897394792)
XLA Ops:
  10.0 6.3 collective-permute-start
  18.2 3.1 collective-permute-start.1
  27.1 6.1 collective-permute-start.3
  34.1 2.4 collective-permute-start.2
  39.8 4.0 collective-permute-start.5
  46.4 3.1 collective-permute-start.8
  51.7 68.0 %while.24 = (s32[]{:T(128)}, f32[24,64,128]{2,1,0:T(8,128)S(1)}, s32[27,24]{1,0:T(8,128)S(1)}, f32[57,64,128]{2,1,0:T(8,128)S(1)}, f32[27,64,64]{2,1,0:T(8,128)}, /*index=5*/s32[]{:T(128)}, s32[]{:T(128)}) while((s32[]{:T(128)}, f32[24,64,128]{2,1,0:T(8,128)S(1)}, s32[27,24]{1,0:T(8,128)S(1)}, f32[57,64,128]{2,1,0:T(8,128)S(1)}, ...), condition=%wide.region_1.2_spmd.clone, body=%wide.region_0.1_spmd.clone.sunk | while | flops 151389264 | bytes 3969511 | solution.py:70
  119.7 2.4 fusion.11
  123.6 237.2 %while.23 = (s32[]{:T(128)}, f32[57,64,128]{2,1,0:T(8,128)}, f32[27,64,64]{2,1,0:T(8,128)}, s32[27,24]{1,0:T(8,128)S(1)}, f32[27,64,64]{2,1,0:T(8,128)}, /*index...) while((s32[]{:T(128)}, f32[57,64,128]{2,1,0:T(8,128)}, f32[27,64,64]{2,1,0:T(8,128)}, ...), condition=%wide.region_4.5_spmd, body=%wide.region_2.4_spmd.sunk | while | flops 302187584 | bytes 7213641 | solution.py:82
  127.3 5.3 scatter_fusion
  136.4 5.0 scatter_fusion
  145.1 5.1 scatter_fusion
  153.9 5.1 scatter_fusion
  162.7 5.0 scatter_fusion
  171.4 5.2 scatter_fusion
  180.3 5.1 scatter_fusion
  189.1 5.1 scatter_fusion
  197.9 5.0 scatter_fusion
  206.5 5.0 scatter_fusion
  215.2 5.0 scatter_fusion
  223.9 5.0 scatter_fusion
  232.6 5.0 scatter_fusion
  241.3 5.0 scatter_fusion
  250.0 5.0 scatter_fusion
  258.7 5.1 scatter_fusion
  267.6 5.1 scatter_fusion
  276.4 5.0 scatter_fusion
  285.0 5.1 scatter_fusion
  293.8 5.0 scatter_fusion
  302.5 5.1 scatter_fusion
  311.3 5.1 scatter_fusion
  320.1 5.1 scatter_fusion
  328.9 5.1 scatter_fusion
  337.7 5.0 scatter_fusion
  346.4 5.3 scatter_fusion
  355.4 5.4 scatter_fusion
  362.2 4.3 collective-permute-start.12
  366.5 6.0 collective-permute-done.12
  376.9 8.2 %collective-permute-start.21 = (f32[4,64,128]{2,1,0:T(8,128)S(1)}, f32[4,64,128]{2,1,0:T(8,128)S(1)}, u32[]{:S(2)}, u32[]{:S(2)}) collective-permute-start(f32[4,64,128]{2,1,0:T(8,128)S(1)} %get-tuple-element.128), channel_id=1, source_target_pairs={{0,8},{8,16},{16,24},{24,32},{32,40},{40,48},{48,56},{56,64},{64,7... | collective-permute-start | bytes 393224 | tf_op jit(solution)/shard_map/ppermute | solution.py:12
  387.0 2.4 collective-permute-start.15
  391.4 3.4 collective-permute-done.15
  394.8 4.1 collective-permute-start.18
  399.0 3.0 collective-permute-start.16
  403.3 6.3 collective-permute-start.23
  411.0 7.7 %collective-permute-done.20 = f32[4,64,128]{2,1,0:T(8,128)S(1)} collective-permute-done((f32[4,64,128]{2,1,0:T(8,128)S(1)}, f32[4,64,128]{2,1,0:T(8,128)S(1)}, u32[]{:S(2)}, u32[]{:S(2)}) %collective-permute-start.20) | collective-permute-done | bytes 131104 | tf_op jit(solution)/shard_map/ppermute | solution.py:12
  418.8 2.1 scatter_fusion.1
  421.0 219.7 %all-reduce.2.cloned.1.call-done = f32[27,64,64]{2,1,0:T(8,128)} async-done(((f32[27,64,64]{2,1,0:T(8,128)}), f32[27,64,64]{2,1,0:T(8,128)}) %all-reduce.2.cloned.1.call-update) | async-done | bytes 442384 | tf_op jit(solution)/shard_map/psum | solution.py:83
  640.7 2.2 copy.58
  (369 shorter events, 198.3 us)
Async XLA Ops:
  7.2 633.5 %all-reduce.2.cloned.1.call-start = ((), (), s32[]{:S(2)}) async-start(), calls=%async_computation | async-start | bytes 1769472 | tf_op jit(solution)/shard_map/psum | solution.py:83
  8.1 25.9 %copy-start.2 = (s32[1,1,24,27]{3,2,1,0:T(8,128)S(1)}, s32[1,1,24,27]{3,2,1,0:T(8,128)}, u32[]{:S(2)}) copy-start(s32[1,1,24,27]{3,2,1,0:T(8,128)} %param.12) | copy-start | bytes 7780
  9.8 41.7 %copy-start.1 = (f32[1,1,24,64,128]{4,3,2,1,0:T(8,128)S(1)}, f32[1,1,24,64,128]{4,3,2,1,0:T(8,128)}, u32[]{:S(2)}) copy-start(f32[1,1,24,64,128]{4,3,2,1,0:T(8,128)} %param.10) | copy-start | bytes 2359300
  10.0 8.3 %collective-permute-start = (f32[4,64,128]{2,1,0:T(8,128)S(1)}, f32[4,64,128]{2,1,0:T(8,128)S(1)}, u32[]{:S(2)}, u32[]{:S(2)}) collective-permute-start(f32[4,64,128]{2,1,0:T(8,128)S(1)} %get-tuple-element.142), channel_id=1, source_target_pairs={{0,8},{8,16},{16,24},{24,32},{32,40},{40,48},{48,56},{56,64},{64,7... | collective-permute-start | bytes 393224 | tf_op jit(solution)/shard_map/ppermute | solution.py:12
  18.2 15.9 %collective-permute-start.1 = (f32[4,64,128]{2,1,0:T(8,128)S(1)}, f32[4,64,128]{2,1,0:T(8,128)S(1)}, u32[]{:S(2)}, u32[]{:S(2)}) collective-permute-start(f32[4,64,128]{2,1,0:T(8,128)S(1)} %collective-permute-done), channel_id=1, source_target_pairs={{0,1},{1,2},{2,3},{3,4},{4,5},{5,6},{6,7},{8,9},{9,10},{10,11},{11... | collective-permute-start | bytes 393224 | tf_op jit(solution)/shard_map/ppermute | solution.py:12
  21.4 18.4 %collective-permute-start.10 = (f32[4,64,128]{2,1,0:T(8,128)S(1)}, f32[4,64,128]{2,1,0:T(8,128)S(1)}, u32[]{:S(2)}, u32[]{:S(2)}) collective-permute-start(f32[4,64,128]{2,1,0:T(8,128)S(1)} %get-tuple-element.135), channel_id=1, source_target_pairs={{8,0},{16,8},{24,16},{32,24},{40,32},{48,40},{56,48},{64,56},{72,6... | collective-permute-start | bytes 393224 | tf_op jit(solution)/shard_map/ppermute | solution.py:12
  23.3 28.2 %collective-permute-start.9 = (f32[4,64,128]{2,1,0:T(8,128)S(1)}, f32[4,64,128]{2,1,0:T(8,128)S(1)}, u32[]{:S(2)}, u32[]{:S(2)}) collective-permute-start(f32[4,64,128]{2,1,0:T(8,128)S(1)} %get-tuple-element.136), channel_id=1, source_target_pairs={{8,0},{16,8},{24,16},{32,24},{40,32},{48,40},{56,48},{64,56},{72,6... | collective-permute-start | bytes 393224 | tf_op jit(solution)/shard_map/ppermute | solution.py:12
  25.2 18.6 %collective-permute-start.7 = (f32[4,64,128]{2,1,0:T(8,128)S(1)}, f32[4,64,128]{2,1,0:T(8,128)S(1)}, u32[]{:S(2)}, u32[]{:S(2)}) collective-permute-start(f32[4,64,128]{2,1,0:T(8,128)S(1)} %get-tuple-element.137), channel_id=1, source_target_pairs={{8,0},{16,8},{24,16},{32,24},{40,32},{48,40},{56,48},{64,56},{72,6... | collective-permute-start | bytes 393224 | tf_op jit(solution)/shard_map/ppermute | solution.py:12
  27.1 9.4 %collective-permute-start.3 = (f32[4,64,128]{2,1,0:T(8,128)S(1)}, f32[4,64,128]{2,1,0:T(8,128)S(1)}, u32[]{:S(2)}, u32[]{:S(2)}) collective-permute-start(f32[4,64,128]{2,1,0:T(8,128)S(1)} %get-tuple-element.140), channel_id=1, source_target_pairs={{0,8},{8,16},{16,24},{24,32},{32,40},{40,48},{48,56},{56,64},{64,7... | collective-permute-start | bytes 393224 | tf_op jit(solution)/shard_map/ppermute | solution.py:12
  34.1 4.3 collective-permute-start.2
  36.6 13.0 %collective-permute-start.6 = (f32[4,64,128]{2,1,0:T(8,128)S(1)}, f32[4,64,128]{2,1,0:T(8,128)S(1)}, u32[]{:S(2)}, u32[]{:S(2)}) collective-permute-start(f32[4,64,128]{2,1,0:T(8,128)S(1)} %get-tuple-element.138), channel_id=1, source_target_pairs={{1,0},{2,1},{3,2},{4,3},{5,4},{6,5},{7,6},{9,8},{10,9},{11,10},{12... | collective-permute-start | bytes 393224 | tf_op jit(solution)/shard_map/ppermute | solution.py:12
  38.5 7.9 %collective-permute-start.4 = (f32[4,64,128]{2,1,0:T(8,128)S(1)}, f32[4,64,128]{2,1,0:T(8,128)S(1)}, u32[]{:S(2)}, u32[]{:S(2)}) collective-permute-start(f32[4,64,128]{2,1,0:T(8,128)S(1)} %collective-permute-done.3), channel_id=1, source_target_pairs={{1,0},{2,1},{3,2},{4,3},{5,4},{6,5},{7,6},{9,8},{10,9},{11,10},{12... | collective-permute-start | bytes 393224 | tf_op jit(solution)/shard_map/ppermute | solution.py:12
  39.8 9.7 %collective-permute-start.5 = (f32[4,64,128]{2,1,0:T(8,128)S(1)}, f32[4,64,128]{2,1,0:T(8,128)S(1)}, u32[]{:S(2)}, u32[]{:S(2)}) collective-permute-start(f32[4,64,128]{2,1,0:T(8,128)S(1)} %get-tuple-element.139), channel_id=1, source_target_pairs={{0,1},{1,2},{2,3},{3,4},{4,5},{5,6},{6,7},{8,9},{9,10},{10,11},{11... | collective-permute-start | bytes 393224 | tf_op jit(solution)/shard_map/ppermute | solution.py:12
  43.8 7.6 %collective-permute-start.11 = (f32[4,64,128]{2,1,0:T(8,128)S(1)}, f32[4,64,128]{2,1,0:T(8,128)S(1)}, u32[]{:S(2)}, u32[]{:S(2)}) collective-permute-start(f32[4,64,128]{2,1,0:T(8,128)S(1)} %collective-permute-done.10), channel_id=1, source_target_pairs={{1,0},{2,1},{3,2},{4,3},{5,4},{6,5},{7,6},{9,8},{10,9},{11,10},{12... | collective-permute-start | bytes 393224 | tf_op jit(solution)/shard_map/ppermute | solution.py:12
  46.4 5.0 collective-permute-start.8
  362.2 10.3 %collective-permute-start.12 = (f32[4,64,128]{2,1,0:T(8,128)S(1)}, f32[4,64,128]{2,1,0:T(8,128)S(1)}, u32[]{:S(2)}, u32[]{:S(2)}) collective-permute-start(f32[4,64,128]{2,1,0:T(8,128)S(1)} %get-tuple-element.134), channel_id=1, source_target_pairs={{8,0},{16,8},{24,16},{32,24},{40,32},{48,40},{56,48},{64,56},{72,6... | collective-permute-start | bytes 393224 | tf_op jit(solution)/shard_map/ppermute | solution.py:12
  372.5 17.0 %collective-permute-start.13 = (f32[4,64,128]{2,1,0:T(8,128)S(1)}, f32[4,64,128]{2,1,0:T(8,128)S(1)}, u32[]{:S(2)}, u32[]{:S(2)}) collective-permute-start(f32[4,64,128]{2,1,0:T(8,128)S(1)} %collective-permute-done.12), channel_id=1, source_target_pairs={{1,0},{2,1},{3,2},{4,3},{5,4},{6,5},{7,6},{9,8},{10,9},{11,10},{12... | collective-permute-start | bytes 393224 | tf_op jit(solution)/shard_map/ppermute | solution.py:12
  375.0 27.0 %collective-permute-start.22 = (f32[4,64,128]{2,1,0:T(8,128)S(1)}, f32[4,64,128]{2,1,0:T(8,128)S(1)}, u32[]{:S(2)}, u32[]{:S(2)}) collective-permute-start(f32[4,64,128]{2,1,0:T(8,128)S(1)} %get-tuple-element.127), channel_id=1, source_target_pairs={{0,8},{8,16},{16,24},{24,32},{32,40},{40,48},{48,56},{56,64},{64,7... | collective-permute-start | bytes 393224 | tf_op jit(solution)/shard_map/ppermute | solution.py:12
  376.9 41.8 %collective-permute-start.21 = (f32[4,64,128]{2,1,0:T(8,128)S(1)}, f32[4,64,128]{2,1,0:T(8,128)S(1)}, u32[]{:S(2)}, u32[]{:S(2)}) collective-permute-start(f32[4,64,128]{2,1,0:T(8,128)S(1)} %get-tuple-element.128), channel_id=1, source_target_pairs={{0,8},{8,16},{16,24},{24,32},{32,40},{40,48},{48,56},{56,64},{64,7... | collective-permute-start | bytes 393224 | tf_op jit(solution)/shard_map/ppermute | solution.py:12
  385.1 18.2 %collective-permute-start.19 = (f32[4,64,128]{2,1,0:T(8,128)S(1)}, f32[4,64,128]{2,1,0:T(8,128)S(1)}, u32[]{:S(2)}, u32[]{:S(2)}) collective-permute-start(f32[4,64,128]{2,1,0:T(8,128)S(1)} %get-tuple-element.129), channel_id=1, source_target_pairs={{0,8},{8,16},{16,24},{24,32},{32,40},{40,48},{48,56},{56,64},{64,7... | collective-permute-start | bytes 393224 | tf_op jit(solution)/shard_map/ppermute | solution.py:12
  387.0 7.8 %collective-permute-start.15 = (f32[4,64,128]{2,1,0:T(8,128)S(1)}, f32[4,64,128]{2,1,0:T(8,128)S(1)}, u32[]{:S(2)}, u32[]{:S(2)}) collective-permute-start(f32[4,64,128]{2,1,0:T(8,128)S(1)} %get-tuple-element.132), channel_id=1, source_target_pairs={{8,0},{16,8},{24,16},{32,24},{40,32},{48,40},{56,48},{64,56},{72,6... | collective-permute-start | bytes 393224 | tf_op jit(solution)/shard_map/ppermute | solution.py:12
  389.5 9.5 %collective-permute-start.14 = (f32[4,64,128]{2,1,0:T(8,128)S(1)}, f32[4,64,128]{2,1,0:T(8,128)S(1)}, u32[]{:S(2)}, u32[]{:S(2)}) collective-permute-start(f32[4,64,128]{2,1,0:T(8,128)S(1)} %get-tuple-element.133), channel_id=1, source_target_pairs={{8,0},{16,8},{24,16},{32,24},{40,32},{48,40},{56,48},{64,56},{72,6... | collective-permute-start | bytes 393224 | tf_op jit(solution)/shard_map/ppermute | solution.py:12
  394.8 16.2 %collective-permute-start.18 = (f32[4,64,128]{2,1,0:T(8,128)S(1)}, f32[4,64,128]{2,1,0:T(8,128)S(1)}, u32[]{:S(2)}, u32[]{:S(2)}) collective-permute-start(f32[4,64,128]{2,1,0:T(8,128)S(1)} %get-tuple-element.130), channel_id=1, source_target_pairs={{0,1},{1,2},{2,3},{3,4},{4,5},{5,6},{6,7},{8,9},{9,10},{10,11},{11... | collective-permute-start | bytes 393224 | tf_op jit(solution)/shard_map/ppermute | solution.py:12
  399.0 10.7 %collective-permute-start.16 = (f32[4,64,128]{2,1,0:T(8,128)S(1)}, f32[4,64,128]{2,1,0:T(8,128)S(1)}, u32[]{:S(2)}, u32[]{:S(2)}) collective-permute-start(f32[4,64,128]{2,1,0:T(8,128)S(1)} %collective-permute-done.15), channel_id=1, source_target_pairs={{0,1},{1,2},{2,3},{3,4},{4,5},{5,6},{6,7},{8,9},{9,10},{10,11},{11... | collective-permute-start | bytes 393224 | tf_op jit(solution)/shard_map/ppermute | solution.py:12
  402.0 9.0 %collective-permute-start.17 = (f32[4,64,128]{2,1,0:T(8,128)S(1)}, f32[4,64,128]{2,1,0:T(8,128)S(1)}, u32[]{:S(2)}, u32[]{:S(2)}) collective-permute-start(f32[4,64,128]{2,1,0:T(8,128)S(1)} %get-tuple-element.131), channel_id=1, source_target_pairs={{1,0},{2,1},{3,2},{4,3},{5,4},{6,5},{7,6},{9,8},{10,9},{11,10},{12... | collective-permute-start | bytes 393224 | tf_op jit(solution)/shard_map/ppermute | solution.py:12
  403.3 15.5 %collective-permute-start.23 = (f32[4,64,128]{2,1,0:T(8,128)S(1)}, f32[4,64,128]{2,1,0:T(8,128)S(1)}, u32[]{:S(2)}, u32[]{:S(2)}) collective-permute-start(f32[4,64,128]{2,1,0:T(8,128)S(1)} %collective-permute-done.22), channel_id=1, source_target_pairs={{0,1},{1,2},{2,3},{3,4},{4,5},{5,6},{6,7},{8,9},{9,10},{10,11},{11... | collective-permute-start | bytes 393224 | tf_op jit(solution)/shard_map/ppermute | solution.py:12
  409.7 9.1 %collective-permute-start.20 = (f32[4,64,128]{2,1,0:T(8,128)S(1)}, f32[4,64,128]{2,1,0:T(8,128)S(1)}, u32[]{:S(2)}, u32[]{:S(2)}) collective-permute-start(f32[4,64,128]{2,1,0:T(8,128)S(1)} %collective-permute-done.19), channel_id=1, source_target_pairs={{1,0},{2,1},{3,2},{4,3},{5,4},{6,5},{7,6},{9,8},{10,9},{11,10},{12... | collective-permute-start | bytes 393224 | tf_op jit(solution)/shard_map/ppermute | solution.py:12
  420.9 221.9 %copy-start = (f32[24,64,128]{2,1,0:T(8,128)}, f32[24,64,128]{2,1,0:T(8,128)S(1)}, u32[]{:S(2)}) copy-start(f32[24,64,128]{2,1,0:T(8,128)S(1)} %scatter_fusion.1) | copy-start | bytes 2359300
Sparse Core Ops, SparseCore 0:
  375.1 265.5 all-reduce.1
where the time goes:
time: 660 us; the launch traced here: 650 us
  waiting for transfers between devices  242 us (37%)
  other arithmetic  143 us (22%)
  matrix products  114 us (17%)
  starting transfers between devices  72.8 us (11%)
  local copies, waits for them, and re-layouts  60.4 us (9%)
  between operations  15.2 us (2%)
    psum x1, waiting for transfers between devices, per_device(): grad_weights = lax.psum(grad_w, ('gx', 'gy'))  220 us
    scatter-add x27, other arithmetic, backward(): return (acc.at[column].add(contrib), g_w)  137 us
    ppermute x24, starting transfers between devices, from_behind(): lax.ppermute(value, axis, [(source, source + steps) for source in range(i...  72.8 us
    dot_general x27, matrix products, forward(): jnp.einsum('oc,tcv->tov', w_k, picked, precision=lax.Precision.HIGHEST)  50.1 us
    dot_general x27, matrix products, backward(): jnp.einsum('oc,tov->tcv', w_k, grad_pre, precision=lax.Precision.HIGHEST)  43.1 us
    ppermute x24, waiting for transfers between devices, from_behind(): lax.ppermute(value, axis, [(source, source + steps) for source in range(i...  22.7 us
    dot_general x27, matrix products, backward(): jnp.einsum('tov,tcv->oc', grad_pre, picked, precision=lax.Precision.HIGHEST)  20.8 us
    dynamic_update_slice x54, local copies, waits for them, and re-layouts, per_device(): lax.scan(backward, jnp.zeros_like(extended), (weights, kmap.T))  18.8 us
  transfers between devices with their start and end apart: 25, of which 8 were waited for; matrix products, arithmetic and copies ran while one was open for 1% of the time, Pallas kernels for 0%

commit v1 on v0

v1 whole, which is shorter than its diff:
```python
import jax
import jax.numpy as jnp
from jax import lax
from jax.experimental import pallas as pl
from jax.experimental.pallas import tpu as pltpu
from jax.sharding import PartitionSpec as P

OFFSETS = ((-1, -1), (-1, 0), (-1, 1), (0, -1), (0, 1), (1, -1), (1, 0), (1, 1))
NX, NY = 32, 8
TILES, HALO, OFFS, C, V = 24, 4, 27, 64, 128
WIDE = TILES + 8 * HALO + 1
KC = 28 * C
NB = KC // 128
GROUP, FAR = 8, 32
MESH = pl.DeviceIdType.MESH
F32, BF16 = jnp.float32, jnp.bfloat16
VMEM = pl.BlockSpec(memory_space=pltpu.VMEM)
SMEM = pl.BlockSpec(memory_space=pltpu.SMEM)


def position():
    return lax.axis_index("gx"), lax.axis_index("gy")


def beside(gx, gy, dx, dy):
    return lax.rem(gx + (dx + NX), NX), lax.rem(gy + (dy + NY), NY)


def inside(gx, gy, dx, dy):
    ok = (gx + dx >= 0) & (gx + dx < NX) & (gy + dy >= 0) & (gy + dy < NY)
    return jnp.where(ok, 1.0, 0.0).astype(F32)


def halves(value):
    high = value.astype(BF16)
    return high, (value - high.astype(F32)).astype(BF16)


def near_rank(gx, gy):
    return lax.rem(gy, 4) * 2 + lax.rem(gx, 2)


def far_rank(gx, gy):
    return (gx // 4) * 4 + lax.rem(gx // 2, 2) * 2 + gy // 4


def device_at(near, far):
    gx = (far // 4) * 4 + lax.rem(far // 2, 2) * 2 + lax.rem(near, 2)
    return gx, lax.rem(far, 2) * 4 + near // 2


def fetch_kernel(sends, feat, weights, xh, xl, wcat, wback, outbox, inbox, send_sem, recv_sem):
    gx, gy = position()
    barrier = pltpu.get_barrier_semaphore()
    for dx, dy in OFFSETS:
        pl.semaphore_signal(barrier, inc=1, device_id=beside(gx, gy, dx, dy), device_id_type=MESH)
    pl.semaphore_wait(barrier, 8)
    copies = []
    for r, (dx, dy) in enumerate(OFFSETS):
        for h in range(HALO):
            outbox[r * HALO + h] = feat[0, 0, sends[0, 0, r, h]]
        copy = pltpu.make_async_remote_copy(
            src_ref=outbox.at[pl.ds(r * HALO, HALO)],
            dst_ref=inbox.at[pl.ds(r * HALO, HALO)],
            send_sem=send_sem.at[r],
            recv_sem=recv_sem.at[r],
            device_id=beside(gx, gy, -dx, -dy),
            device_id_type=MESH,
        )
        copy.start()
        copies.append(copy)

    def split_tile(t, carry):
        xh[t], xl[t] = halves(feat[0, 0, t])
        return carry

    lax.fori_loop(0, TILES, split_tile, 0)
    xh[WIDE - 1] = jnp.zeros((C, V), BF16)
    xl[WIDE - 1] = jnp.zeros((C, V), BF16)
    for m in range(NB):
        left = weights[2 * m]
        right = weights[2 * m + 1] if 2 * m + 1 < OFFS else jnp.zeros((C, C), F32)
        pair = jnp.concatenate([left, right], axis=1)
        high, low = halves(pair)
        wcat[0:C, m * 128 : m * 128 + 128] = high
        wcat[C : 2 * C, m * 128 : m * 128 + 128] = low
        turned = pair.T
        high = turned.astype(BF16).astype(F32)
        both = jnp.concatenate([high, turned - high], axis=1).astype(BF16)
        wback[m * 128 : m * 128 + 128, 0:128] = both
        wback[m * 128 : m * 128 + 128, 128:256] = both
    for r, (dx, dy) in enumerate(OFFSETS):
        copies[r].wait_recv()
        there = inside(gx, gy, dx, dy)
        for h in range(HALO):
            slot = r * HALO + h
            xh[TILES + slot], xl[TILES + slot] = halves(inbox[slot] * there)
    for copy in copies:
        copy.wait_send()


def tile_kernel(kmap, counts, xh, xl, wcat, wback, cot, act, ge, gw, catch, catl, total):
    ge[...] = jnp.zeros_like(ge)
    total[...] = jnp.zeros_like(total)
    catch[OFFS * C : KC, :] = jnp.zeros((C, 2 * V), BF16)
    catl[OFFS * C : KC, :] = jnp.zeros((C, 2 * V), BF16)
    contract_last = (((1,), (1,)), ((), ()))

    def pair(p, carry):
        slots = [[kmap[0, 0, 2 * p + h, k] for h in range(2)] for k in range(OFFS)]
        for k in range(OFFS):
            for h in range(2):
                catch[k * C : k * C + C, h * V : h * V + V] = xh[slots[k][h]]
                catl[k * C : k * C + C, h * V : h * V + V] = xl[slots[k][h]]
        first = jnp.dot(wcat[...], catch[...], preferred_element_type=F32)
        second = jnp.dot(wcat[0:C, :], catl[...], preferred_element_type=F32)
        pre = first[0:C] + first[C:] + second
        sig = jax.nn.sigmoid(pre)
        slope = sig * (1.0 + pre * (1.0 - sig))
        value = pre * sig
        grads = []
        for h in range(2):
            live = jnp.where(2 * p + h < counts[0, 0], 1.0, 0.0).astype(F32)
            act[2 * p + h] = value[:, h * V : h * V + V] * live
            grads.append(cot[0, 0, 2 * p + h] * live * slope[:, h * V : h * V + V])
        gh, gl = halves(jnp.concatenate(grads, axis=1))
        two = lax.dot_general(
            jnp.concatenate([gh, gl], axis=0), catch[...], contract_last, preferred_element_type=F32
        )
        one = lax.dot_general(gh, catl[...], contract_last, preferred_element_type=F32)
        total[...] += two[0:C] + two[C:] + one
        four = jnp.concatenate([gh, gh, gl, gl], axis=0)
        for k in range(OFFS):
            part = jnp.dot(wback[k * C : k * C + C, :], four, preferred_element_type=F32)
            for h in range(2):
                ge[slots[k][h]] += part[:, h * V : h * V + V]
        return carry

    lax.fori_loop(0, TILES // 2, pair, 0)
    for j in range(GROUP):
        gw[j] = total[j * 8 : j * 8 + 8, :]


def return_kernel(ge, gw, back, out, near_in, part, far_in, full, halo_s, halo_r, near_s, near_r, far_s, far_r, spread_s, spread_r, end_s, end_r):
    gx, gy = position()
    near, far = near_rank(gx, gy), far_rank(gx, gy)

    def near_device(d):
        return device_at(lax.rem(near + d, GROUP), far)

    def far_device(d):
        return device_at(near, lax.rem(far + d, FAR))

    barrier = pltpu.get_barrier_semaphore()

    def greet_near(d, carry):
        pl.semaphore_signal(barrier, inc=1, device_id=near_device(d), device_id_type=MESH)
        return carry

    def greet_far(d, carry):
        pl.semaphore_signal(barrier, inc=1, device_id=far_device(d), device_id_type=MESH)
        return carry

    for dx, dy in OFFSETS:
        pl.semaphore_signal(barrier, inc=1, device_id=beside(gx, gy, dx, dy), device_id_type=MESH)
    lax.fori_loop(1, GROUP, greet_near, 0)
    lax.fori_loop(1, FAR, greet_far, 0)
    pl.semaphore_wait(barrier, 8 + GROUP - 1 + FAR - 1)

    def near_copy(d):
        return pltpu.make_async_remote_copy(
            src_ref=gw.at[lax.rem(near + d, GROUP)],
            dst_ref=near_in.at[d],
            send_sem=near_s.at[d],
            recv_sem=near_r.at[d],
            device_id=near_device(d),
            device_id_type=MESH,
        )

    def far_copy(d):
        return pltpu.make_async_remote_copy(
            src_ref=part.at[lax.rem(far + d, FAR) // 2],
            dst_ref=far_in.at[d],
            send_sem=far_s.at[d],
            recv_sem=far_r.at[d],
            device_id=far_device(d),
            device_id_type=MESH,
        )

    def spread_copy(d, i):
        return pltpu.make_async_remote_copy(
            src_ref=full.at[i],
            dst_ref=full.at[i],
            send_sem=spread_s.at[d],
            recv_sem=spread_r.at[i],
            device_id=far_device(d),
            device_id_type=MESH,
        )

    def end_copy(d):
        return pltpu.make_async_remote_copy(
            src_ref=full,
            dst_ref=out.at[near],
            send_sem=end_s.at[d],
            recv_sem=end_r.at[d],
            device_id=near_device(d),
            device_id_type=MESH,
        )

    def reduces(rank):
        return (lax.rem(rank, 2) == 0) & (rank < 2 * NB)

    def each(low, high, act):
        def step(d, carry):
            act(d)
            return carry

        lax.fori_loop(low, high, step, 0)

    each(1, GROUP, lambda d: near_copy(d).start())
    halo = []
    for r, (dx, dy) in enumerate(OFFSETS):
        copy = pltpu.make_async_remote_copy(
            src_ref=ge.at[pl.ds(TILES + r * HALO, HALO)],
            dst_ref=back.at[pl.ds(r * HALO, HALO)],
            send_sem=halo_s.at[r],
            recv_sem=halo_r.at[r],
            device_id=beside(gx, gy, dx, dy),
            device_id_type=MESH,
        )
        copy.start()
        halo.append(copy)

    each(1, GROUP, lambda d: near_copy(d).wait_recv())
    mine = gw[near]
    for d in range(1, GROUP):
        mine = mine + near_in[d]
    for i in range(NB):
        part[i] = mine[:, i * 128 : i * 128 + 128]

    def if_other_reduces(d, act):
        pl.when(reduces(lax.rem(far + d, FAR)))(act)

    each(1, FAR, lambda d: if_other_reduces(d, lambda: far_copy(d).start()))

    own = lax.rem(far // 2, NB)

    @pl.when(reduces(far))
    def _():
        each(1, FAR, lambda d: far_copy(d).wait_recv())

        def add(d, acc):
            return acc + far_in[d]

        full[own] = lax.fori_loop(1, FAR, add, part[own])
        each(1, FAR, lambda d: spread_copy(d, own).start())

    def arrived(i):
        pl.when(2 * i != far)(lambda: spread_copy(1, i).wait_recv())

    each(0, NB, arrived)
    each(1, GROUP, lambda d: end_copy(d).start())
    out[near] = full[...]
    each(1, GROUP, lambda d: near_copy(d).wait_send())
    each(1, FAR, lambda d: if_other_reduces(d, lambda: far_copy(d).wait_send()))
    pl.when(reduces(far))(lambda: each(1, FAR, lambda d: spread_copy(d, own).wait_send()))
    for copy in halo:
        copy.wait()
    each(1, GROUP, lambda d: end_copy(d).wait())


def finish_kernel(sends, ge, back, summed, gf, gwo):
    gx, gy = position()
    gf[...] = ge[0:TILES]
    for r, (dx, dy) in enumerate(OFFSETS):
        there = inside(gx, gy, -dx, -dy)
        for h in range(HALO):
            gf[sends[0, 0, r, h]] += back[r * HALO + h] * there
    for j in range(GROUP):
        for i in range(NB):
            block = summed[j, i]
            gwo[2 * i, j * 8 : j * 8 + 8, :] = block[:, 0:C]
            if 2 * i + 1 < OFFS:
                gwo[2 * i + 1, j * 8 : j * 8 + 8, :] = block[:, C : 2 * C]


def shaped(shape, dtype=F32):
    return jax.ShapeDtypeStruct(shape, dtype)


def run_tiles(kernel_map, counts, xh, xl, wcat, wback, cotangent):
    return pl.pallas_call(
        tile_kernel,
        out_shape=(shaped((TILES, C, V)), shaped((WIDE, C, V)), shaped((GROUP, 8, KC))),
        in_specs=[SMEM, SMEM] + [VMEM] * 5,
        out_specs=(VMEM,) * 3,
        scratch_shapes=[
            pltpu.VMEM((KC, 2 * V), BF16),
            pltpu.VMEM((KC, 2 * V), BF16),
            pltpu.VMEM((C, KC), F32),
        ],
        compiler_params=pltpu.CompilerParams(vmem_limit_bytes=32 << 20),
    )(kernel_map, counts, xh, xl, wcat, wback, cotangent)


def per_device(features, weights, kernel_map, send_lists, counts, cotangent):
    dma = pltpu.SemaphoreType.DMA
    xh, xl, wcat, wback = pl.pallas_call(
        fetch_kernel,
        out_shape=(
            shaped((WIDE, C, V), BF16),
            shaped((WIDE, C, V), BF16),
            shaped((2 * C, KC), BF16),
            shaped((KC, 4 * C), BF16),
        ),
        in_specs=[SMEM, VMEM, VMEM],
        out_specs=(VMEM,) * 4,
        scratch_shapes=[
            pltpu.VMEM((8 * HALO, C, V), F32),
            pltpu.VMEM((8 * HALO, C, V), F32),
            dma((8,)),
            dma((8,)),
        ],
        compiler_params=pltpu.CompilerParams(collective_id=0, has_side_effects=True, vmem_limit_bytes=24 << 20),
    )(send_lists, features, weights)
    act, ge, gw = run_tiles(kernel_map, counts, xh, xl, wcat, wback, cotangent)
    back, summed = pl.pallas_call(
        return_kernel,
        out_shape=(shaped((8 * HALO, C, V)), shaped((GROUP, NB, 8, 128))),
        in_specs=[VMEM, VMEM],
        out_specs=(VMEM, VMEM),
        scratch_shapes=[
            pltpu.VMEM((GROUP, 8, KC), F32),
            pltpu.VMEM((16, 8, 128), F32),
            pltpu.VMEM((FAR, 8, 128), F32),
            pltpu.VMEM((NB, 8, 128), F32),
            dma((8,)),
            dma((8,)),
            dma((GROUP,)),
            dma((GROUP,)),
            dma((FAR,)),
            dma((FAR,)),
            dma((FAR,)),
            dma((NB,)),
            dma((GROUP,)),
            dma((GROUP,)),
        ],
        compiler_params=pltpu.CompilerParams(collective_id=1, has_side_effects=True, vmem_limit_bytes=24 << 20),
    )(ge, gw)
    gf, gwo = pl.pallas_call(
        finish_kernel,
        out_shape=(shaped((TILES, C, V)), shaped((OFFS, C, C))),
        in_specs=[SMEM, VMEM, VMEM, VMEM],
        out_specs=(VMEM, VMEM),
        compiler_params=pltpu.CompilerParams(vmem_limit_bytes=24 << 20),
    )(send_lists, ge, back, summed)
    return act[None, None], gf[None, None], gwo


def solution(mesh):
    placed = (
        P("gx", "gy", None, None, None),
        P(),
        P("gx", "gy", None, None),
        P("gx", "gy", None, None),
        P("gx", "gy"),
        P("gx", "gy", None, None, None),
    )
    return jax.shard_map(
        per_device,
        mesh=mesh,
        in_specs=placed,
        out_specs=(P("gx", "gy", None, None, None), P("gx", "gy", None, None, None), P()),
        check_vma=False,
    )
```

time: 660 us -> 93.7 us (0.14); the launches traced: 650 us -> 93.5 us
  waiting for transfers between devices: 242 us -> 0 us
  other arithmetic: 143 us -> 0 us
  matrix products: 114 us -> 0 us
  Pallas kernels: 0 us -> 88.4 us
  starting transfers between devices: 72.8 us -> 0 us
  local copies, waits for them, and re-layouts: 60.4 us -> 3.76 us
  between operations: 15.2 us -> 1.31 us
    psum x1 -> x0, waiting for transfers between devices: 220 us -> none  [per_device(): grad_weights = lax.psum(grad_w, ('gx', 'gy'))]
    scatter-add x28 -> x0, other arithmetic: 139 us -> none  [the longest x27 137 us: backward(): return (acc.at[column].add(contrib), g_w)]
    dot_general x81 -> x0, matrix products: 114 us -> none  [the longest x27 50.1 us: forward(): jnp.einsum('oc,tcv->tov', w_k, picked, precision=lax.Precision.HIGHEST)]
    pallas_call x0 -> x4, Pallas kernels: none -> 88.4 us  [the longest x1 38.4 us: per_device(): pl.pallas_call(return_kernel, out_shape=(shaped((8 * HALO, C, V)), shaped...]
    ppermute x24 -> x0, starting transfers between devices: 72.8 us -> none  [from_behind(): lax.ppermute(value, axis, [(source, source + steps) for source in range(i...]
    gather x55 -> x0, local copies, waits for them, and re-layouts: 34.1 us -> none  [the longest x27 16.2 us: forward(): picked = extended[column]]
    ppermute x24 -> x0, waiting for transfers between devices: 22.7 us -> none  [from_behind(): lax.ppermute(value, axis, [(source, source + steps) for source in range(i...]
    dynamic_update_slice x54 -> x0, local copies, waits for them, and re-layouts: 18.8 us -> none  [per_device(): lax.scan(backward, jnp.zeros_like(extended), (weights, kmap.T))]
  transfers between devices with their start and end apart: 25 -> 0, of which waited for: 8 -> 0; matrix products, arithmetic and copies ran while one was open for 1% -> 0% of each run, Pallas kernels for 0% -> 0%
where the time goes in v1:
time: 93.7 us; the launch traced here: 93.5 us
  Pallas kernels  88.4 us (94%)
  local copies, waits for them, and re-layouts  3.76 us (4%)
  between operations  1.31 us (1%)
    pallas_call x1, Pallas kernels, per_device(): pl.pallas_call(return_kernel, out_shape=(shaped((8 * HALO, C, V)), shaped...  38.4 us
    pallas_call x1, Pallas kernels, run_tiles(): pl.pallas_call(tile_kernel, out_shape=(shaped((TILES, C, V)), shaped((WID...  25.9 us
    pallas_call x1, Pallas kernels, per_device(): pl.pallas_call(fetch_kernel, out_shape=(shaped((WIDE, C, V), BF16), shape...  22.2 us
    unnamed x9, local copies, waits for them, and re-layouts  3.76 us
    pallas_call x1, Pallas kernels, per_device(): pl.pallas_call(finish_kernel, out_shape=(shaped((TILES, C, V)), shaped((O...  2 us

profile of v1, /device:TPU:1, one launch (start us, length us, event | category | flops | bytes accessed | tf_op | source)
XLA Modules:
  0.0 93.5 jit_solution(2759114313267072318)
XLA Ops:
  1.3 0.8 copy.9.sends
  2.0 0.0 copy-start
  2.0 1.2 %copy-done = f32[27,64,64]{2,1,0:T(8,128)S(1)} copy-done((f32[27,64,64]{2,1,0:T(8,128)S(1)}, f32[27,64,64]{2,1,0:T(8,128)}, u32[]{:S(2)}) %copy-start) | copy-done | bytes 442392
  3.2 0.0 copy-start.2
  3.2 1.1 %copy-done.2 = f32[1,1,24,64,128]{4,3,2,1,0:T(8,128)S(1)} copy-done((f32[1,1,24,64,128]{4,3,2,1,0:T(8,128)S(1)}, f32[1,1,24,64,128]{4,3,2,1,0:T(8,128)}, u32[]{:S(2)}) %copy-start.2) | copy-done | bytes 786456
  4.3 0.0 copy-start.1
  4.3 22.2 %shard_map.85 = (bf16[57,64,128]{2,1,0:T(8,128)(2,1)S(1)}, bf16[57,64,128]{2,1,0:T(8,128)(2,1)S(1)}, bf16[128,1792]{1,0:T(8,128)(2,1)S(1)}, bf16[1792,256]{1,0:T(8,128)(2,1)S(1)}) custom-call(s32[1,1,8,4]{3,2,1,0:T(8,128)S(1)} %copy.9.sends, f32[1,1,24,64,128]{4,3,2,1,0:T(8,128)S(1)} %copy-done.2, f32[27,64,64]{2,1,0:T(8,128)S(1)} %copy-done), custom_call_target="tpu_custom_call" | custom-call | tf_op jit(solution)/shard_map/pallas_call | solution.py:308
  26.5 0.0 copy-done.1
  26.5 0.0 copy-start.3
  26.6 0.7 copy-done.3
  27.3 25.9 %shard_map.86 = (f32[24,64,128]{2,1,0:T(8,128)}, f32[57,64,128]{2,1,0:T(8,128)S(1)}, f32[8,8,1792]{2,1,0:T(8,128)S(1)}) custom-call(s32[1,1,24,27]{3,2,1,0:T(8,128)S(1)} %copy-done.3, s32[1,1]{1,0:T(1,128)S(6)} %copy.11.counts, bf16[57,64,128]{2,1,0:T(8,128)(2,1)S(1)} %get-tuple-element.14.xh, bf16[57,64,128]{2,1,0:T(8,128)(2,1)S(1)} %get-tuple-element.15.xl, ...), custom_call_target="tpu_custom_call" | custom-call | tf_op jit(solution)/shard_map/pallas_call | solution.py:292
  53.1 38.4 %shard_map.87 = (f32[32,64,128]{2,1,0:T(8,128)S(1)}, f32[8,14,8,128]{3,2,1,0:T(8,128)S(1)}) custom-call(f32[57,64,128]{2,1,0:T(8,128)S(1)} %get-tuple-element.19.ge, f32[8,8,1792]{2,1,0:T(8,128)S(1)} %get-tuple-element.20.gw), custom_call_target="tpu_custom_call" | custom-call | tf_op jit(solution)/shard_map/pallas_call | solution.py:327
  91.5 2.0 %shard_map.88 = (f32[24,64,128]{2,1,0:T(8,128)}, f32[27,64,64]{2,1,0:T(8,128)}) custom-call(s32[1,1,8,4]{3,2,1,0:T(8,128)S(1)} %copy.9.sends, f32[57,64,128]{2,1,0:T(8,128)S(1)} %get-tuple-element.19.ge, f32[32,64,128]{2,1,0:T(8,128)S(1)} %get-tuple-element.21.back, f32[8,14,8,128]{3,2,1,0:T(8,128)S(1)} %get-tuple-element.22.summed), custom_call_target="tpu_custom_call" | custom-call | tf_op jit(solution)/shard_map/pallas_call | solution.py:350
Async XLA Ops:
  2.0 1.2 %copy-start = (f32[27,64,64]{2,1,0:T(8,128)S(1)}, f32[27,64,64]{2,1,0:T(8,128)}, u32[]{:S(2)}) copy-start(f32[27,64,64]{2,1,0:T(8,128)} %weights.1) | copy-start | bytes 1327108
  3.2 1.1 %copy-start.2 = (f32[1,1,24,64,128]{4,3,2,1,0:T(8,128)S(1)}, f32[1,1,24,64,128]{4,3,2,1,0:T(8,128)}, u32[]{:S(2)}) copy-start(f32[1,1,24,64,128]{4,3,2,1,0:T(8,128)} %feat.1) | copy-start | bytes 2359300
  4.3 22.2 %copy-start.1 = (f32[1,1,24,64,128]{4,3,2,1,0:T(8,128)S(1)}, f32[1,1,24,64,128]{4,3,2,1,0:T(8,128)}, u32[]{:S(2)}) copy-start(f32[1,1,24,64,128]{4,3,2,1,0:T(8,128)} %cot.1) | copy-start | bytes 2359300
  26.5 0.7 copy-start.3

commit v2 on v1

v2 whole, which is shorter than its diff:
```python
import jax
import jax.numpy as jnp
from jax import lax
from jax.experimental import pallas as pl
from jax.experimental.pallas import tpu as pltpu
from jax.sharding import PartitionSpec as P

OFFSETS = ((-1, -1), (-1, 0), (-1, 1), (0, -1), (0, 1), (1, -1), (1, 0), (1, 1))
NX, NY = 32, 8
TILES, HALO, OFFS, C, V = 24, 4, 27, 64, 128
WIDE = TILES + 8 * HALO + 1
KC = 28 * C
NB = KC // 128
PLANE, DEEP, PAIRS = 16, 8, 2
MESH = pl.DeviceIdType.MESH
F32, BF16 = jnp.float32, jnp.bfloat16
VMEM = pl.BlockSpec(memory_space=pltpu.VMEM)
ANY = pl.BlockSpec(memory_space=pl.ANY)
SMEM = pl.BlockSpec(memory_space=pltpu.SMEM)


def position():
    return lax.axis_index("gx"), lax.axis_index("gy")


def beside(gx, gy, dx, dy):
    return lax.rem(gx + (dx + NX), NX), lax.rem(gy + (dy + NY), NY)


def inside(gx, gy, dx, dy):
    ok = (gx + dx >= 0) & (gx + dx < NX) & (gy + dy >= 0) & (gy + dy < NY)
    return jnp.where(ok, 1.0, 0.0).astype(F32)


def halves(value):
    high = value.astype(BF16)
    return high, (value - high.astype(F32)).astype(BF16)


def fetch_kernel(sends, feat_hbm, weights_hbm, xh, xl, wcat, wback, feat, weights, outbox, inbox, load_sem, send_sem, recv_sem):
    gx, gy = position()
    load_feat = pltpu.make_async_copy(feat_hbm.at[0, 0], feat, load_sem.at[0])
    load_weights = pltpu.make_async_copy(weights_hbm, weights, load_sem.at[1])
    load_feat.start()
    load_weights.start()
    barrier = pltpu.get_barrier_semaphore()
    for dx, dy in OFFSETS:
        pl.semaphore_signal(barrier, inc=1, device_id=beside(gx, gy, dx, dy), device_id_type=MESH)
    load_feat.wait()
    for r in range(8):
        for h in range(HALO):
            outbox[r * HALO + h] = feat[sends[0, 0, r, h]]
    pl.semaphore_wait(barrier, 8)
    copies = []
    for r, (dx, dy) in enumerate(OFFSETS):
        copy = pltpu.make_async_remote_copy(
            src_ref=outbox.at[pl.ds(r * HALO, HALO)],
            dst_ref=inbox.at[pl.ds(r * HALO, HALO)],
            send_sem=send_sem.at[r],
            recv_sem=recv_sem.at[r],
            device_id=beside(gx, gy, -dx, -dy),
            device_id_type=MESH,
        )
        copy.start()
        copies.append(copy)
    load_weights.wait()

    def split_tile(t, carry):
        xh[t], xl[t] = halves(feat[t])
        return carry

    lax.fori_loop(0, TILES, split_tile, 0)
    xh[WIDE - 1] = jnp.zeros((C, V), BF16)
    xl[WIDE - 1] = jnp.zeros((C, V), BF16)
    for m in range(NB):
        left = weights[2 * m]
        right = weights[2 * m + 1] if 2 * m + 1 < OFFS else jnp.zeros((C, C), F32)
        pair = jnp.concatenate([left, right], axis=1)
        high, low = halves(pair)
        wcat[0:C, m * 128 : m * 128 + 128] = high
        wcat[C : 2 * C, m * 128 : m * 128 + 128] = low
        turned = pair.T
        high = turned.astype(BF16).astype(F32)
        both = jnp.concatenate([high, turned - high], axis=1).astype(BF16)
        wback[m * 128 : m * 128 + 128, 0:128] = both
        wback[m * 128 : m * 128 + 128, 128:256] = both
    for r, (dx, dy) in enumerate(OFFSETS):
        copies[r].wait_recv()
        there = inside(gx, gy, dx, dy)
        for h in range(HALO):
            slot = r * HALO + h
            xh[TILES + slot], xl[TILES + slot] = halves(inbox[slot] * there)
    for copy in copies:
        copy.wait_send()


def tile_kernel(kmap, counts, xh, xl, wcat, wback, cot, act, ge, g2, catch, catl):
    ge[...] = jnp.zeros_like(ge)
    for q in range(PAIRS):
        catch[q, OFFS * C : KC, :] = jnp.zeros((C, 2 * V), BF16)
        catl[q, OFFS * C : KC, :] = jnp.zeros((C, 2 * V), BF16)

    def step(p, carry):
        def tile(q, h):
            return (p * PAIRS + q) * 2 + h

        slots = [[[kmap[0, 0, tile(q, h), k] for h in range(2)] for k in range(OFFS)] for q in range(PAIRS)]
        for q in range(PAIRS):
            for k in range(OFFS):
                for h in range(2):
                    catch[q, k * C : k * C + C, h * V : h * V + V] = xh[slots[q][k][h]]
                    catl[q, k * C : k * C + C, h * V : h * V + V] = xl[slots[q][k][h]]
        sums = []
        for q in range(PAIRS):
            first = jnp.dot(wcat[...], catch[q], preferred_element_type=F32)
            second = jnp.dot(wcat[0:C, :], catl[q], preferred_element_type=F32)
            sums.append(first[0:C] + first[C:] + second)
        fours = []
        for q in range(PAIRS):
            pre = sums[q]
            sig = jax.nn.sigmoid(pre)
            slope = sig * (1.0 + pre * (1.0 - sig))
            value = pre * sig
            grads = []
            for h in range(2):
                live = jnp.where(tile(q, h) < counts[0, 0], 1.0, 0.0).astype(F32)
                act[tile(q, h)] = value[:, h * V : h * V + V] * live
                grads.append(cot[0, 0, tile(q, h)] * live * slope[:, h * V : h * V + V])
            gh, gl = halves(jnp.concatenate(grads, axis=1))
            lanes = pl.ds(pl.multiple_of((p * PAIRS + q) * 2 * V, 2 * V), 2 * V)
            g2[0:C, lanes] = gh
            g2[C : 2 * C, lanes] = gl
            fours.append(jnp.concatenate([gh, gh, gl, gl], axis=0))
        for q in range(PAIRS):
            for k in range(OFFS):
                part = jnp.dot(wback[k * C : k * C + C, :], fours[q], preferred_element_type=F32)
                for h in range(2):
                    ge[slots[q][k][h]] += part[:, h * V : h * V + V]
        return carry

    lax.fori_loop(0, TILES // (2 * PAIRS), step, 0)


def return_kernel(kmap, xh, xl, g2, ge, back, out, cath, catl, mine, theirs, given, summed, xy_in, z_in, half, halo_s, halo_r, core_s, core_r, xy_s, xy_r, z_s, z_r, spread_s, spread_r, end_s, end_r):
    gx, gy = position()
    core, z = lax.rem(gx, 2), gx // 4
    xy = (lax.rem(gx // 2, 2) * 2 + gy // 4) * 4 + lax.rem(gy, 4)

    def xy_device(u):
        return (z * 4 + (u // 8) * 2 + core, lax.rem(u // 4, 2) * 4 + lax.rem(u, 4))

    def z_device(d):
        return (lax.rem(z + d, DEEP) * 4 + lax.rem(gx, 4), gy)

    other = (gx + 1 - 2 * core, gy)
    barrier = pltpu.get_barrier_semaphore()

    def greet(device):
        pl.semaphore_signal(barrier, inc=1, device_id=device, device_id_type=MESH)

    for dx, dy in OFFSETS:
        greet(beside(gx, gy, dx, dy))
    greet(other)
    for u in range(PLANE):
        pl.when(xy != u)(lambda u=u: greet(xy_device(u)))
    for d in range(1, DEEP):
        greet(z_device(d))

    def send(src, dst, send_sem, recv_sem, device):
        return pltpu.make_async_remote_copy(
            src_ref=src, dst_ref=dst, send_sem=send_sem, recv_sem=recv_sem, device_id=device, device_id_type=MESH
        )

    def core_copy(n):
        return send(theirs.at[n], given.at[n], core_s.at[n], core_r.at[n], other)

    def xy_copy(m, source, target):
        return send(summed.at[m], xy_in.at[source], xy_s.at[m], xy_r.at[source], xy_device(target))

    def z_copy(d, slot):
        return send(z_in.at[slot], z_in.at[slot], z_s.at[d], z_r.at[slot], z_device(d))

    def spread_copy(m, target):
        return send(half.at[m], half.at[m], spread_s.at[target], spread_r.at[m], xy_device(target))

    def compute(n):
        for kk in range(4):
            k = jnp.minimum(4 * n + kk, OFFS - 1)
            for t in range(TILES):
                slot = kmap[0, 0, t, k]
                cath[kk * C : kk * C + C, t * V : t * V + V] = xh[slot]
                catl[kk * C : kk * C + C, t * V : t * V + V] = xl[slot]
        contract_last = (((1,), (1,)), ((), ()))
        two = lax.dot_general(g2[...], cath[...], contract_last, preferred_element_type=F32)
        one = lax.dot_general(g2[0:C, :], catl[...], contract_last, preferred_element_type=F32)
        total = two[0:C] + two[C:] + one

        @pl.when(core == 0)
        def _():
            mine[n] = total[0:32]
            theirs[n] = total[32:64]

        @pl.when(core == 1)
        def _():
            mine[n] = total[32:64]
            theirs[n] = total[0:32]

    def pass_on(n):
        core_copy(n).wait_recv()
        both = mine[n] + given[n]
        for e in range(2):
            m = 2 * n + e
            summed[m] = both[:, e * 128 : e * 128 + 128]
            pl.when(xy != m)(lambda m=m: xy_copy(m, xy, m).start())

    compute(0)
    pl.semaphore_wait(barrier, 8 + 1 + PLANE - 1 + DEEP - 1)
    core_copy(0).start()
    halo = []
    for r, (dx, dy) in enumerate(OFFSETS):
        copy = send(
            ge.at[pl.ds(TILES + r * HALO, HALO)],
            back.at[pl.ds(r * HALO, HALO)],
            halo_s.at[r],
            halo_r.at[r],
            beside(gx, gy, dx, dy),
        )
        copy.start()
        halo.append(copy)

    def stage(n, carry):
        compute(n)
        core_copy(n).start()
        pass_on(n - 1)
        return carry

    lax.fori_loop(1, NB // 2, stage, 0)
    pass_on(NB // 2 - 1)

    reducer = xy < NB
    own = jnp.minimum(xy, NB - 1)

    @pl.when(reducer)
    def _():
        xy_in[xy] = summed[own]
        for u in range(PLANE):
            pl.when(xy != u)(lambda u=u: xy_copy(0, u, 0).wait_recv())
        acc = xy_in[0]
        for u in range(1, PLANE):
            acc = acc + xy_in[u]
        z_in[z] = acc
        for d in range(1, DEEP):
            z_copy(d, z).start()
        for d in range(1, DEEP):
            z_copy(d, lax.rem(z + d, DEEP)).wait_recv()
        acc = z_in[0]
        for d in range(1, DEEP):
            acc = acc + z_in[d]
        half[own] = acc
        for u in range(PLANE):
            pl.when(xy != u)(lambda u=u: spread_copy(own, u).start())

    for m in range(NB):
        pl.when(xy != m)(lambda m=m: spread_copy(m, 0).wait_recv())
    end = send(half, out.at[core], end_s, end_r, other)
    end.start()
    out[core] = half[...]
    for n in range(NB // 2):
        core_copy(n).wait_send()
    for m in range(NB):
        pl.when(xy != m)(lambda m=m: xy_copy(m, xy, m).wait_send())

    @pl.when(reducer)
    def _():
        for d in range(1, DEEP):
            z_copy(d, z).wait_send()
        for u in range(PLANE):
            pl.when(xy != u)(lambda u=u: spread_copy(own, u).wait_send())

    for copy in halo:
        copy.wait()
    end.wait()


def finish_kernel(sends, ge, back, summed, gf, gwo):
    gx, gy = position()
    gf[...] = ge[...]
    for r, (dx, dy) in enumerate(OFFSETS):
        there = inside(gx, gy, -dx, -dy)
        for h in range(HALO):
            gf[sends[0, 0, r, h]] += back[r * HALO + h] * there
    for c in range(2):
        for m in range(NB):
            block = summed[c, m]
            gwo[2 * m, c * 32 : c * 32 + 32, :] = block[:, 0:C]
            if 2 * m + 1 < OFFS:
                gwo[2 * m + 1, c * 32 : c * 32 + 32, :] = block[:, C : 2 * C]


def shaped(shape, dtype=F32):
    return jax.ShapeDtypeStruct(shape, dtype)


def run_tiles(kernel_map, counts, xh, xl, wcat, wback, cotangent):
    return pl.pallas_call(
        tile_kernel,
        out_shape=(shaped((TILES, C, V)), shaped((WIDE, C, V)), shaped((2 * C, TILES * V), BF16)),
        in_specs=[SMEM, SMEM] + [VMEM] * 5,
        out_specs=(VMEM,) * 3,
        scratch_shapes=[
            pltpu.VMEM((PAIRS, KC, 2 * V), BF16),
            pltpu.VMEM((PAIRS, KC, 2 * V), BF16),
        ],
        compiler_params=pltpu.CompilerParams(vmem_limit_bytes=32 << 20),
    )(kernel_map, counts, xh, xl, wcat, wback, cotangent)


def per_device(features, weights, kernel_map, send_lists, counts, cotangent):
    dma = pltpu.SemaphoreType.DMA
    xh, xl, wcat, wback = pl.pallas_call(
        fetch_kernel,
        out_shape=(
            shaped((WIDE, C, V), BF16),
            shaped((WIDE, C, V), BF16),
            shaped((2 * C, KC), BF16),
            shaped((KC, 4 * C), BF16),
        ),
        in_specs=[SMEM, ANY, ANY],
        out_specs=(VMEM,) * 4,
        scratch_shapes=[
            pltpu.VMEM((TILES, C, V), F32),
            pltpu.VMEM((OFFS, C, C), F32),
            pltpu.VMEM((8 * HALO, C, V), F32),
            pltpu.VMEM((8 * HALO, C, V), F32),
            dma((2,)),
            dma((8,)),
            dma((8,)),
        ],
        compiler_params=pltpu.CompilerParams(collective_id=0, has_side_effects=True, vmem_limit_bytes=24 << 20),
    )(send_lists, features, weights)
    act, ge, g2 = run_tiles(kernel_map, counts, xh, xl, wcat, wback, cotangent)
    back, summed = pl.pallas_call(
        return_kernel,
        out_shape=(shaped((8 * HALO, C, V)), shaped((2, NB, 32, 128))),
        in_specs=[SMEM, VMEM, VMEM, VMEM, ANY],
        out_specs=(ANY, VMEM),
        scratch_shapes=[
            pltpu.VMEM((4 * C, TILES * V), BF16),
            pltpu.VMEM((4 * C, TILES * V), BF16),
            pltpu.VMEM((NB // 2, 32, 256), F32),
            pltpu.VMEM((NB // 2, 32, 256), F32),
            pltpu.VMEM((NB // 2, 32, 256), F32),
            pltpu.VMEM((NB, 32, 128), F32),
            pltpu.VMEM((PLANE, 32, 128), F32),
            pltpu.VMEM((DEEP, 32, 128), F32),
            pltpu.VMEM((NB, 32, 128), F32),
            dma((8,)),
            dma((8,)),
            dma((NB // 2,)),
            dma((NB // 2,)),
            dma((NB,)),
            dma((PLANE,)),
            dma((DEEP,)),
            dma((DEEP,)),
            dma((PLANE,)),
            dma((NB,)),
            dma,
            dma,
        ],
        compiler_params=pltpu.CompilerParams(collective_id=1, has_side_effects=True, vmem_limit_bytes=24 << 20),
    )(kernel_map, xh, xl, g2, ge)
    gf, gwo = pl.pallas_call(
        finish_kernel,
        out_shape=(shaped((TILES, C, V)), shaped((OFFS, C, C))),
        grid=(1,),
        in_specs=[SMEM, pl.BlockSpec((TILES, C, V), lambda i: (0, 0, 0)), VMEM, VMEM],
        out_specs=(VMEM, VMEM),
        compiler_params=pltpu.CompilerParams(vmem_limit_bytes=24 << 20),
    )(send_lists, ge, back, summed)
    return act[None, None], gf[None, None], gwo


def solution(mesh):
    placed = (
        P("gx", "gy", None, None, None),
        P(),
        P("gx", "gy", None, None),
        P("gx", "gy", None, None),
        P("gx", "gy"),
        P("gx", "gy", None, None, None),
    )
    return jax.shard_map(
        per_device,
        mesh=mesh,
        in_specs=placed,
        out_specs=(P("gx", "gy", None, None, None), P("gx", "gy", None, None, None), P()),
        check_vma=False,
    )
```

time: 93.7 us -> 84.2 us (0.90)
  Pallas kernels: 88.4 us -> 78.9 us
    pallas_call x1, Pallas kernels: 25.9 us -> 17.4 us  [run_tiles(): pl.pallas_call(tile_kernel, out_shape=(shaped((TILES, C, V)), shaped((WID...]
    pallas_call x1, Pallas kernels: 38.4 us -> 37 us  [per_device(): pl.pallas_call(return_kernel, out_shape=(shaped((8 * HALO, C, V)), shaped...]
where the time goes in v2:
time: 84.2 us; the launch traced here: 83.9 us
  Pallas kernels  78.9 us (94%)
  local copies, waits for them, and re-layouts  3.76 us (4%)
  between operations  1.31 us (2%)
    pallas_call x1, Pallas kernels, per_device(): pl.pallas_call(return_kernel, out_shape=(shaped((8 * HALO, C, V)), shaped...  37 us
    pallas_call x1, Pallas kernels, per_device(): pl.pallas_call(fetch_kernel, out_shape=(shaped((WIDE, C, V), BF16), shape...  22.5 us
    pallas_call x1, Pallas kernels, run_tiles(): pl.pallas_call(tile_kernel, out_shape=(shaped((TILES, C, V)), shaped((WID...  17.4 us
    unnamed x9, local copies, waits for them, and re-layouts  3.76 us
    pallas_call x1, Pallas kernels, per_device(): pl.pallas_call(finish_kernel, out_shape=(shaped((TILES, C, V)), shaped((O...  1.99 us

profile of v2, /device:TPU:1, one launch (start us, length us, event | category | flops | bytes accessed | tf_op | source)
XLA Modules:
  0.0 83.9 jit_solution(6163920033264073183)
XLA Ops:
  1.3 0.8 copy.9.sends
  2.0 0.0 copy-start
  2.0 1.2 %copy-done = f32[27,64,64]{2,1,0:T(8,128)S(1)} copy-done((f32[27,64,64]{2,1,0:T(8,128)S(1)}, f32[27,64,64]{2,1,0:T(8,128)}, u32[]{:S(2)}) %copy-start) | copy-done | bytes 442392
  3.2 0.0 copy-start.2
  3.2 1.1 %copy-done.2 = f32[1,1,24,64,128]{4,3,2,1,0:T(8,128)S(1)} copy-done((f32[1,1,24,64,128]{4,3,2,1,0:T(8,128)S(1)}, f32[1,1,24,64,128]{4,3,2,1,0:T(8,128)}, u32[]{:S(2)}) %copy-start.2) | copy-done | bytes 786456
  4.3 0.0 copy-start.1
  4.3 22.5 %shard_map.85 = (bf16[57,64,128]{2,1,0:T(8,128)(2,1)S(1)}, bf16[57,64,128]{2,1,0:T(8,128)(2,1)S(1)}, bf16[128,1792]{1,0:T(8,128)(2,1)S(1)}, bf16[1792,256]{1,0:T(8,128)(2,1)S(1)}) custom-call(s32[1,1,8,4]{3,2,1,0:T(8,128)S(1)} %copy.9.sends, f32[1,1,24,64,128]{4,3,2,1,0:T(8,128)S(1)} %copy-done.2, f32[27,64,64]{2,1,0:T(8,128)S(1)} %copy-done), custom_call_target="tpu_custom_call" | custom-call | tf_op jit(solution)/shard_map/pallas_call | solution.py:320
  26.8 0.0 copy-done.1
  26.8 0.0 copy-start.3
  26.8 0.7 copy-done.3
  27.5 17.4 %shard_map.86 = (f32[24,64,128]{2,1,0:T(8,128)}, f32[57,64,128]{2,1,0:T(8,128)S(1)}, bf16[128,3072]{1,0:T(8,128)(2,1)S(1)}) custom-call(s32[1,1,24,27]{3,2,1,0:T(8,128)S(1)} %copy-done.3, s32[1,1]{1,0:T(1,128)S(6)} %copy.11.counts, bf16[57,64,128]{2,1,0:T(8,128)(2,1)S(1)} %get-tuple-element.14.xh, bf16[57,64,128]{2,1,0:T(8,128)(2,1)S(1)} %get-tuple-element.15.xl, ...), custom_call_target="tpu_custom_call" | custom-call | tf_op jit(solution)/shard_map/pallas_call | solution.py:305
  45.0 37.0 %shard_map.87 = (f32[32,64,128]{2,1,0:T(8,128)S(1)}, f32[2,14,32,128]{3,2,1,0:T(8,128)S(1)}) custom-call(s32[1,1,24,27]{3,2,1,0:T(8,128)S(1)} %copy-done.3, bf16[57,64,128]{2,1,0:T(8,128)(2,1)S(1)} %get-tuple-element.14.xh, bf16[57,64,128]{2,1,0:T(8,128)(2,1)S(1)} %get-tuple-element.15.xl, bf16[128,3072]{1,0:T(8,128)(2,1)S(1)} %get-tuple-element.20.g2, ...), custom_call_target="tpu_custom_call" | custom-call | tf_op jit(solution)/shard_map/pallas_call | solution.py:342
  82.0 2.0 %shard_map.88 = (f32[24,64,128]{2,1,0:T(8,128)}, f32[27,64,64]{2,1,0:T(8,128)}) custom-call(s32[1,1,8,4]{3,2,1,0:T(8,128)S(1)} %copy.9.sends, f32[57,64,128]{2,1,0:T(8,128)S(1)} %get-tuple-element.19.ge, f32[32,64,128]{2,1,0:T(8,128)S(1)} %get-tuple-element.21.back, f32[2,14,32,128]{3,2,1,0:T(8,128)S(1)} %get-tuple-element.22.summed), custom_call_target="tpu_custom_call" | custom-call | tf_op jit(solution)/shard_map/pallas_call | solution.py:372
Async XLA Ops:
  2.0 1.2 %copy-start = (f32[27,64,64]{2,1,0:T(8,128)S(1)}, f32[27,64,64]{2,1,0:T(8,128)}, u32[]{:S(2)}) copy-start(f32[27,64,64]{2,1,0:T(8,128)} %weights_hbm.1) | copy-start | bytes 1327108
  3.2 1.1 %copy-start.2 = (f32[1,1,24,64,128]{4,3,2,1,0:T(8,128)S(1)}, f32[1,1,24,64,128]{4,3,2,1,0:T(8,128)}, u32[]{:S(2)}) copy-start(f32[1,1,24,64,128]{4,3,2,1,0:T(8,128)} %feat_hbm.1) | copy-start | bytes 2359300
  4.3 22.5 %copy-start.1 = (f32[1,1,24,64,128]{4,3,2,1,0:T(8,128)S(1)}, f32[1,1,24,64,128]{4,3,2,1,0:T(8,128)}, u32[]{:S(2)}) copy-start(f32[1,1,24,64,128]{4,3,2,1,0:T(8,128)} %cot.1) | copy-start | bytes 2359300
  26.8 0.7 copy-start.3

commit v3 on v0

v3 whole, which is shorter than its diff:
```python
import jax
import jax.numpy as jnp
from jax import lax
from jax.experimental import pallas as pl
from jax.experimental.pallas import tpu as pltpu
from jax.sharding import PartitionSpec as P

OFFSETS = ((-1, -1), (-1, 0), (-1, 1), (0, -1), (0, 1), (1, -1), (1, 0), (1, 1))
NX, NY = 32, 8
TILES, HALO, OFFS, C, V = 24, 4, 27, 64, 128
WIDE = TILES + 8 * HALO + 1
KC = 28 * C
NB = KC // 128
PLANE, DEEP = 16, 8
QUAD = 4
ENTRIES = TILES * OFFS
RANKS = 768
MESH = pl.DeviceIdType.MESH
F32, BF16 = jnp.float32, jnp.bfloat16
VMEM = pl.BlockSpec(memory_space=pltpu.VMEM)
ANY = pl.BlockSpec(memory_space=pl.ANY)
SMEM = pl.BlockSpec(memory_space=pltpu.SMEM)


def position():
    return lax.axis_index("gx"), lax.axis_index("gy")


def beside(gx, gy, dx, dy):
    return lax.rem(gx + (dx + NX), NX), lax.rem(gy + (dy + NY), NY)


def inside(gx, gy, dx, dy):
    ok = (gx + dx >= 0) & (gx + dx < NX) & (gy + dy >= 0) & (gy + dy < NY)
    return jnp.where(ok, 1.0, 0.0).astype(F32)


def halves(value):
    high = value.astype(BF16)
    return high, (value - high.astype(F32)).astype(BF16)


def main_kernel(
    kmap,
    sends,
    counts,
    kmap_rows,
    feat_hbm,
    weights_hbm,
    cot_hbm,
    act,
    ge,
    back,
    out,
    feat,
    weights,
    cot,
    xh,
    xl,
    wcat,
    wback,
    box,
    inbox,
    catch,
    catl,
    total,
    stacked,
    parts,
    runs,
    order_v,
    upto_v,
    order,
    upto,
    mine,
    theirs,
    given,
    summed,
    xy_in,
    z_in,
    half,
    load_sem,
    table_sem,
    in_s,
    in_r,
    halo_s,
    halo_r,
    core_s,
    core_r,
    xy_s,
    xy_r,
    z_s,
    z_r,
    spread_s,
    spread_r,
    end_s,
    end_r,
):
    gx, gy = position()
    core, z = lax.rem(gx, 2), gx // 4
    xy = (lax.rem(gx // 2, 2) * 2 + gy // 4) * 4 + lax.rem(gy, 4)

    def xy_device(u):
        return (z * 4 + (u // 8) * 2 + core, lax.rem(u // 4, 2) * 4 + lax.rem(u, 4))

    def z_device(d):
        return (lax.rem(z + d, DEEP) * 4 + lax.rem(gx, 4), gy)

    other = (gx + 1 - 2 * core, gy)
    load_feat = pltpu.make_async_copy(feat_hbm.at[0, 0], feat, load_sem.at[0])
    load_weights = pltpu.make_async_copy(weights_hbm, weights, load_sem.at[1])
    load_cot = pltpu.make_async_copy(cot_hbm.at[0, 0], cot, load_sem.at[2])
    load_feat.start()
    load_weights.start()
    load_cot.start()
    barrier = pltpu.get_barrier_semaphore()

    def greet(device):
        pl.semaphore_signal(barrier, inc=1, device_id=device, device_id_type=MESH)

    for d in range(1, DEEP):
        greet(z_device(d))
    for dx, dy in OFFSETS:
        greet(beside(gx, gy, dx, dy))
    for u in range(PLANE):
        pl.when(xy != u)(lambda u=u: greet(xy_device(u)))
    greet(other)

    def send(src, dst, send_sem, recv_sem, device):
        return pltpu.make_async_remote_copy(
            src_ref=src, dst_ref=dst, send_sem=send_sem, recv_sem=recv_sem, device_id=device, device_id_type=MESH
        )

    load_feat.wait()
    for r in range(8):
        for h in range(HALO):
            box[r * HALO + h] = feat[sends[0, 0, r, h]]
    load_weights.wait()
    for m in range(NB):
        left = weights[2 * m]
        right = weights[2 * m + 1] if 2 * m + 1 < OFFS else jnp.zeros((C, C), F32)
        pair = jnp.concatenate([left, right], axis=1)
        high, low = halves(pair)
        wcat[0:C, m * 128 : m * 128 + 128] = high
        wcat[C : 2 * C, m * 128 : m * 128 + 128] = low
        turned = pair.T
        high = turned.astype(BF16).astype(F32)
        both = jnp.concatenate([high, turned - high], axis=1).astype(BF16)
        wback[m * 128 : m * 128 + 128, 0:128] = both
        wback[m * 128 : m * 128 + 128, 128:256] = both

    pl.semaphore_wait(barrier, 8 + 1 + PLANE - 1 + DEEP - 1)
    arriving = []
    for r, (dx, dy) in enumerate(OFFSETS):
        block = pl.ds(r * HALO, HALO)
        copy = send(box.at[block], inbox.at[block], in_s.at[r], in_r.at[r], beside(gx, gy, -dx, -dy))
        copy.start()
        arriving.append(copy)

    def split_tile(t, carry):
        xh[t], xl[t] = halves(feat[t])
        return carry

    lax.fori_loop(0, TILES, split_tile, 0)
    xh[WIDE - 1] = jnp.zeros((C, V), BF16)
    xl[WIDE - 1] = jnp.zeros((C, V), BF16)
    total[...] = jnp.zeros_like(total)
    catch[OFFS * C : KC, :] = jnp.zeros((C, QUAD * V), BF16)
    catl[OFFS * C : KC, :] = jnp.zeros((C, QUAD * V), BF16)

    place = lax.broadcasted_iota(jnp.int32, (TILES, OFFS), 0) * OFFS + lax.broadcasted_iota(jnp.int32, (TILES, OFFS), 1)
    keys = kmap_rows[0, 0] * 1024 + place
    lanes = lax.broadcasted_iota(jnp.int32, (8, 128), 1)

    def rank_row(t, carry):
        ranks, below = carry
        for k in range(OFFS):
            entry = kmap[0, 0, t, k]
            ranks = ranks + jnp.where(keys > entry * 1024 + (t * OFFS + k), 1, 0)
            below = below + jnp.where(lanes >= entry, 1, 0)
        return ranks, below

    ranks, below = lax.fori_loop(
        0, TILES, rank_row, (jnp.zeros((TILES, OFFS), jnp.int32), jnp.zeros((8, 128), jnp.int32))
    )
    upto_v[...] = below
    spots = lax.broadcasted_iota(jnp.int32, (TILES, RANKS), 1)
    found = jnp.zeros((TILES, RANKS), jnp.int32)
    for k in range(OFFS):
        found = found + jnp.where(ranks[:, k : k + 1] == spots, keys[:, k : k + 1], 0)
    order_v[...] = jnp.broadcast_to(jnp.sum(found, axis=0, keepdims=True), (8, RANKS))
    tables = [
        pltpu.make_async_copy(order_v, order, table_sem.at[0]),
        pltpu.make_async_copy(upto_v, upto, table_sem.at[1]),
    ]
    for table in tables:
        table.start()
    load_cot.wait()
    for r, (dx, dy) in enumerate(OFFSETS):
        arriving[r].wait_recv()
        there = inside(gx, gy, dx, dy)
        for h in range(HALO):
            slot = r * HALO + h
            xh[TILES + slot], xl[TILES + slot] = halves(inbox[slot] * there)
    for copy in arriving:
        copy.wait_send()
    for table in tables:
        table.wait()

    contract_last = (((1,), (1,)), ((), ()))

    def forward(p, carry):
        for k in range(OFFS):
            for h in range(QUAD):
                slot = kmap[0, 0, p * QUAD + h, k]
                catch[k * C : k * C + C, h * V : h * V + V] = xh[slot]
                catl[k * C : k * C + C, h * V : h * V + V] = xl[slot]
        first = jnp.dot(wcat[...], catch[...], preferred_element_type=F32)
        second = jnp.dot(wcat[0:C, :], catl[...], preferred_element_type=F32)
        pre = first[0:C] + first[C:] + second
        sig = jax.nn.sigmoid(pre)
        slope = sig * (1.0 + pre * (1.0 - sig))
        value = pre * sig
        grads = []
        for h in range(QUAD):
            tile = p * QUAD + h
            live = jnp.where(tile < counts[0, 0], 1.0, 0.0).astype(F32)
            act[tile] = value[:, h * V : h * V + V] * live
            grads.append(cot[tile] * live * slope[:, h * V : h * V + V])
        gh, gl = halves(jnp.concatenate(grads, axis=1))
        stacked[p, 0:C] = gh
        stacked[p, C : 2 * C] = gl
        two = lax.dot_general(
            jnp.concatenate([gh, gl], axis=0), catch[...], contract_last, preferred_element_type=F32
        )
        one = lax.dot_general(gh, catl[...], contract_last, preferred_element_type=F32)
        total[...] += two[0:C] + two[C:] + one
        return carry

    lax.fori_loop(0, TILES // QUAD, forward, 0)

    core_copy = send(theirs, given, core_s, core_r, other)

    def xy_copy(m, source, target):
        return send(summed.at[m], xy_in.at[source], xy_s.at[m], xy_r.at[source], xy_device(target))

    def z_copy(d, slot):
        return send(z_in.at[slot], z_in.at[slot], z_s.at[d], z_r.at[slot], z_device(d))

    def spread_copy(m, target):
        return send(half.at[m], half.at[m], spread_s.at[target], spread_r.at[m], xy_device(target))

    reducer = xy < NB
    own = jnp.minimum(xy, NB - 1)
    for c in range(2):

        @pl.when(core == c)
        def _(c=c):
            for m in range(NB):
                mine[m] = total[c * 32 : c * 32 + 32, m * 128 : m * 128 + 128]
                theirs[m] = total[32 - c * 32 : 64 - c * 32, m * 128 : m * 128 + 128]

    core_copy.start()

    def backward(p, carry):
        gh = stacked[p, 0:C]
        gl = stacked[p, C : 2 * C]
        four = jnp.concatenate([gh, gh, gl, gl], axis=0)
        for k in range(OFFS):
            part = jnp.dot(wback[k * C : k * C + C, :], four, preferred_element_type=F32)
            for h in range(QUAD):
                parts[(p * QUAD + h) * OFFS + k] = part[:, h * V : h * V + V]
        return carry

    lax.fori_loop(0, 2, backward, 0)
    core_copy.wait_recv()
    for m in range(NB):
        summed[m] = mine[m] + given[m]
    for m in range(NB):
        pl.when(xy != m)(lambda m=m: xy_copy(m, xy, m).start())
    lax.fori_loop(2, TILES // QUAD, backward, 0)

    @pl.when(reducer)
    def _():
        xy_in[xy] = summed[own]
        for u in range(PLANE):
            pl.when(xy != u)(lambda u=u: xy_copy(0, u, 0).wait_recv())
        acc = xy_in[0]
        for u in range(1, PLANE):
            acc = acc + xy_in[u]
        z_in[z] = acc
        for d in range(1, DEEP):
            z_copy(d, z).start()

    def scan(step, carry):
        acc, last = carry
        for i in range(8):
            spot = step * 8 + i
            key = order[0, spot]
            entry = lax.shift_right_logical(key, 10)
            same = jnp.where(entry == last, 1.0, 0.0).astype(F32)
            acc = acc * same + parts[lax.bitwise_and(key, 1023)]
            runs[spot] = acc
            last = entry
        return acc, last

    lax.fori_loop(0, ENTRIES // 8, scan, (jnp.zeros((C, V), F32), jnp.int32(WIDE)))

    def gathered(entry):
        stop = upto[0, entry]
        begin = upto[0, entry - 1] if entry > 0 else jnp.int32(0)
        return runs[jnp.maximum(stop - 1, 0)] * jnp.where(stop > begin, 1.0, 0.0).astype(F32)

    leaving = []
    for r, (dx, dy) in enumerate(OFFSETS):
        for h in range(HALO):
            box[r * HALO + h] = gathered(TILES + r * HALO + h)
        block = pl.ds(r * HALO, HALO)
        copy = send(box.at[block], back.at[block], halo_s.at[r], halo_r.at[r], beside(gx, gy, dx, dy))
        copy.start()
        leaving.append(copy)

    @pl.when(reducer)
    def _():
        for d in range(1, DEEP):
            z_copy(d, lax.rem(z + d, DEEP)).wait_recv()
        acc = z_in[0]
        for d in range(1, DEEP):
            acc = acc + z_in[d]
        half[own] = acc
        for u in range(PLANE):
            pl.when(xy != u)(lambda u=u: spread_copy(own, u).start())

    for t in range(TILES):
        ge[t] = gathered(t)
    for m in range(NB):
        pl.when(xy != m)(lambda m=m: spread_copy(m, 0).wait_recv())
    end = send(half, out.at[core], end_s, end_r, other)
    end.start()
    out[core] = half[...]
    core_copy.wait_send()
    for m in range(NB):
        pl.when(xy != m)(lambda m=m: xy_copy(m, xy, m).wait_send())

    @pl.when(reducer)
    def _():
        for d in range(1, DEEP):
            z_copy(d, z).wait_send()
        for u in range(PLANE):
            pl.when(xy != u)(lambda u=u: spread_copy(own, u).wait_send())

    for copy in leaving:
        copy.wait()
    end.wait()


def finish_kernel(sends, ge, back, summed, act, acts, gf, gwo):
    gx, gy = position()
    acts[...] = act[...]
    gf[...] = ge[...]
    for r, (dx, dy) in enumerate(OFFSETS):
        there = inside(gx, gy, -dx, -dy)
        for h in range(HALO):
            gf[sends[0, 0, r, h]] += back[r * HALO + h] * there
    for c in range(2):
        for m in range(NB):
            block = summed[c, m]
            gwo[2 * m, c * 32 : c * 32 + 32, :] = block[:, 0:C]
            if 2 * m + 1 < OFFS:
                gwo[2 * m + 1, c * 32 : c * 32 + 32, :] = block[:, C : 2 * C]


def shaped(shape, dtype=F32):
    return jax.ShapeDtypeStruct(shape, dtype)


def per_device(features, weights, kernel_map, send_lists, counts, cotangent):
    dma = pltpu.SemaphoreType.DMA
    vmem = pltpu.VMEM
    act, ge, back, summed = pl.pallas_call(
        main_kernel,
        out_shape=(
            shaped((TILES, C, V)),
            shaped((TILES, C, V)),
            shaped((8 * HALO, C, V)),
            shaped((2, NB, 32, 128)),
        ),
        in_specs=[SMEM, SMEM, SMEM, VMEM, ANY, ANY, ANY],
        out_specs=(VMEM, VMEM, ANY, VMEM),
        scratch_shapes=[
            vmem((TILES, C, V), F32),
            vmem((OFFS, C, C), F32),
            vmem((TILES, C, V), F32),
            vmem((WIDE, C, V), BF16),
            vmem((WIDE, C, V), BF16),
            vmem((2 * C, KC), BF16),
            vmem((KC, 4 * C), BF16),
            vmem((8 * HALO, C, V), F32),
            vmem((8 * HALO, C, V), F32),
            vmem((KC, QUAD * V), BF16),
            vmem((KC, QUAD * V), BF16),
            vmem((C, KC), F32),
            vmem((TILES // QUAD, 2 * C, QUAD * V), BF16),
            vmem((ENTRIES, C, V), F32),
            vmem((ENTRIES, C, V), F32),
            vmem((8, RANKS), jnp.int32),
            vmem((8, 128), jnp.int32),
            pltpu.SMEM((8, RANKS), jnp.int32),
            pltpu.SMEM((8, 128), jnp.int32),
            vmem((NB, 32, 128), F32),
            vmem((NB, 32, 128), F32),
            vmem((NB, 32, 128), F32),
            vmem((NB, 32, 128), F32),
            vmem((PLANE, 32, 128), F32),
            vmem((DEEP, 32, 128), F32),
            vmem((NB, 32, 128), F32),
            dma((3,)),
            dma((2,)),
            dma((8,)),
            dma((8,)),
            dma((8,)),
            dma((8,)),
            dma,
            dma,
            dma((NB,)),
            dma((PLANE,)),
            dma((DEEP,)),
            dma((DEEP,)),
            dma((PLANE,)),
            dma((NB,)),
            dma,
            dma,
        ],
        compiler_params=pltpu.CompilerParams(collective_id=0, has_side_effects=True, vmem_limit_bytes=60 << 20),
    )(kernel_map, send_lists, counts, kernel_map, features, weights, cotangent)
    act, gf, gwo = pl.pallas_call(
        finish_kernel,
        out_shape=(shaped((TILES, C, V)), shaped((TILES, C, V)), shaped((OFFS, C, C))),
        in_specs=[SMEM, VMEM, VMEM, VMEM, VMEM],
        out_specs=(VMEM, VMEM, VMEM),
        compiler_params=pltpu.CompilerParams(vmem_limit_bytes=24 << 20),
    )(send_lists, ge, back, summed, act)
    return act[None, None], gf[None, None], gwo


def solution(mesh):
    placed = (
        P("gx", "gy", None, None, None),
        P(),
        P("gx", "gy", None, None),
        P("gx", "gy", None, None),
        P("gx", "gy"),
        P("gx", "gy", None, None, None),
    )
    return jax.shard_map(
        per_device,
        mesh=mesh,
        in_specs=placed,
        out_specs=(P("gx", "gy", None, None, None), P("gx", "gy", None, None, None), P()),
        check_vma=False,
    )
```

time: 660 us -> 81.6 us (0.12); the launches traced: 650 us -> 81.2 us
  waiting for transfers between devices: 242 us -> 0 us
  other arithmetic: 143 us -> 0 us
  matrix products: 114 us -> 0 us
  Pallas kernels: 0 us -> 73.4 us
  starting transfers between devices: 72.8 us -> 0 us
  local copies, waits for them, and re-layouts: 60.4 us -> 6.54 us
  between operations: 15.2 us -> 1.3 us
    psum x1 -> x0, waiting for transfers between devices: 220 us -> none  [per_device(): grad_weights = lax.psum(grad_w, ('gx', 'gy'))]
    scatter-add x28 -> x0, other arithmetic: 139 us -> none  [the longest x27 137 us: backward(): return (acc.at[column].add(contrib), g_w)]
    dot_general x81 -> x0, matrix products: 114 us -> none  [the longest x27 50.1 us: forward(): jnp.einsum('oc,tcv->tov', w_k, picked, precision=lax.Precision.HIGHEST)]
    pallas_call x0 -> x2, Pallas kernels: none -> 73.4 us  [the longest x1 71.1 us: per_device(): pl.pallas_call(main_kernel, out_shape=(shaped((TILES, C, V)), shaped((TIL...]
    ppermute x24 -> x0, starting transfers between devices: 72.8 us -> none  [from_behind(): lax.ppermute(value, axis, [(source, source + steps) for source in range(i...]
    gather x55 -> x0, local copies, waits for them, and re-layouts: 34.1 us -> none  [the longest x27 16.2 us: forward(): picked = extended[column]]
    ppermute x24 -> x0, waiting for transfers between devices: 22.7 us -> none  [from_behind(): lax.ppermute(value, axis, [(source, source + steps) for source in range(i...]
    dynamic_update_slice x54 -> x0, local copies, waits for them, and re-layouts: 18.8 us -> none  [per_device(): lax.scan(backward, jnp.zeros_like(extended), (weights, kmap.T))]
  transfers between devices with their start and end apart: 25 -> 0, of which waited for: 8 -> 0; matrix products, arithmetic and copies ran while one was open for 1% -> 0% of each run, Pallas kernels for 0% -> 0%
where the time goes in v3:
time: 81.6 us; the launch traced here: 81.2 us
  Pallas kernels  73.4 us (90%)
  local copies, waits for them, and re-layouts  6.54 us (8%)
  between operations  1.3 us (2%)
    pallas_call x1, Pallas kernels, per_device(): pl.pallas_call(main_kernel, out_shape=(shaped((TILES, C, V)), shaped((TIL...  71.1 us
    unnamed x11, local copies, waits for them, and re-layouts  6.54 us
    pallas_call x1, Pallas kernels, per_device(): pl.pallas_call(finish_kernel, out_shape=(shaped((TILES, C, V)), shaped((T...  2.31 us

profile of v3, /device:TPU:1, one launch (start us, length us, event | category | flops | bytes accessed | tf_op | source)
XLA Modules:
  0.0 81.2 jit_solution(15091153561990682886)
XLA Ops:
  1.3 1.3 %copy.10.sends = s32[1,1,8,4]{3,2,1,0:T(8,128)} copy(s32[1,1,8,4]{2,3,1,0:T(4,128)} %param.9) | data formatting | bytes 256 | tf_op args[3]
  2.6 71.1 %shard_map.85 = (f32[24,64,128]{2,1,0:T(8,128)}, f32[24,64,128]{2,1,0:T(8,128)}, f32[32,64,128]{2,1,0:T(8,128)}, f32[2,14,32,128]{3,2,1,0:T(8,128)}) custom-call(s32[1,1,24,27]{3,2,1,0:T(8,128)} %kmap_rows.1, s32[1,1,8,4]{3,2,1,0:T(8,128)} %copy.10.sends, s32[1,1]{1,0:T(1,128)S(6)} %copy.11.counts, s32[1,1,24,27]{3,2,1,0:T(8,128)} %kmap_rows.1, ...), custom_call_target="tpu_custom_call" | custom-call | tf_op jit(solution)/shard_map/pallas_call | solution.py:379
  73.7 0.0 copy-start.4
  73.7 0.7 copy-done.4
  74.4 0.0 copy-start
  74.4 1.2 %copy-done = f32[32,64,128]{2,1,0:T(8,128)S(1)} copy-done((f32[32,64,128]{2,1,0:T(8,128)S(1)}, f32[32,64,128]{2,1,0:T(8,128)}, u32[]{:S(2)}) %copy-start) | copy-done | bytes 1048600
  75.6 0.0 copy-start.1
  75.6 1.1 %copy-done.1 = f32[24,64,128]{2,1,0:T(8,128)S(1)} copy-done((f32[24,64,128]{2,1,0:T(8,128)S(1)}, f32[24,64,128]{2,1,0:T(8,128)}, u32[]{:S(2)}) %copy-start.1) | copy-done | bytes 786456
  76.8 0.0 copy-start.2
  76.8 1.1 %copy-done.2 = f32[24,64,128]{2,1,0:T(8,128)S(1)} copy-done((f32[24,64,128]{2,1,0:T(8,128)S(1)}, f32[24,64,128]{2,1,0:T(8,128)}, u32[]{:S(2)}) %copy-start.2) | copy-done | bytes 786456
  77.9 0.0 copy-start.3
  77.9 1.0 %copy-done.3 = f32[2,14,32,128]{3,2,1,0:T(8,128)S(1)} copy-done((f32[2,14,32,128]{3,2,1,0:T(8,128)S(1)}, f32[2,14,32,128]{3,2,1,0:T(8,128)}, u32[]{:S(2)}) %copy-start.3) | copy-done | bytes 458776
  78.9 2.3 %shard_map.86 = (f32[24,64,128]{2,1,0:T(8,128)}, f32[24,64,128]{2,1,0:T(8,128)}, f32[27,64,64]{2,1,0:T(8,128)}) custom-call(s32[1,1,8,4]{3,2,1,0:T(8,128)S(1)} %copy-done.4, f32[24,64,128]{2,1,0:T(8,128)S(1)} %copy-done.2, f32[32,64,128]{2,1,0:T(8,128)S(1)} %copy-done, f32[2,14,32,128]{3,2,1,0:T(8,128)S(1)} %copy-done.3, f32[24,64,128]{2,1,0:T(8,128)S(1)} %copy-done.1), custom_call_target="tpu_custom_call" | custom-call | tf_op jit(solution)/shard_map/pallas_call | solution.py:435
Async XLA Ops:
  73.7 0.7 copy-start.4
  74.4 1.2 %copy-start = (f32[32,64,128]{2,1,0:T(8,128)S(1)}, f32[32,64,128]{2,1,0:T(8,128)}, u32[]{:S(2)}) copy-start(f32[32,64,128]{2,1,0:T(8,128)} %get-tuple-element.11.back) | copy-start | bytes 3145732
  75.6 1.1 %copy-start.1 = (f32[24,64,128]{2,1,0:T(8,128)S(1)}, f32[24,64,128]{2,1,0:T(8,128)}, u32[]{:S(2)}) copy-start(f32[24,64,128]{2,1,0:T(8,128)} %get-tuple-element.13.act) | copy-start | bytes 2359300
  76.8 1.1 %copy-start.2 = (f32[24,64,128]{2,1,0:T(8,128)S(1)}, f32[24,64,128]{2,1,0:T(8,128)}, u32[]{:S(2)}) copy-start(f32[24,64,128]{2,1,0:T(8,128)} %get-tuple-element.10.ge) | copy-start | bytes 2359300
  77.9 1.0 %copy-start.3 = (f32[2,14,32,128]{3,2,1,0:T(8,128)S(1)}, f32[2,14,32,128]{3,2,1,0:T(8,128)}, u32[]{:S(2)}) copy-start(f32[2,14,32,128]{3,2,1,0:T(8,128)} %get-tuple-element.12.summed) | copy-start | bytes 1376260

commit v4 on v3

--- a/solution.py
+++ b/solution.py
@@ -15,6 +15,7 @@
 QUAD = 4
 ENTRIES = TILES * OFFS
 RANKS = 768
+PIECE = 56
 MESH = pl.DeviceIdType.MESH
 F32, BF16 = jnp.float32, jnp.bfloat16
 VMEM = pl.BlockSpec(memory_space=pltpu.VMEM)
@@ -48,8 +49,8 @@
     feat_hbm,
     weights_hbm,
     cot_hbm,
-    act,
-    ge,
+    act_hbm,
+    ge_hbm,
     back,
     out,
     feat,
@@ -79,6 +80,7 @@
     z_in,
     half,
     load_sem,
+    store_sem,
     table_sem,
     in_s,
     in_r,
@@ -88,8 +90,8 @@
     core_r,
     xy_s,
     xy_r,
-    z_s,
-    z_r,
+    fold_s,
+    fold_r,
     spread_s,
     spread_r,
     end_s,
@@ -133,7 +135,15 @@
     load_feat.wait()
     for r in range(8):
         for h in range(HALO):
-            box[r * HALO + h] = feat[sends[0, 0, r, h]]
+            box[r * HALO + h] = feat[sends[0, 0, h, r]]
+    pl.semaphore_wait(barrier, 8 + 1 + PLANE - 1 + DEEP - 1)
+    arriving = []
+    for r, (dx, dy) in enumerate(OFFSETS):
+        block = pl.ds(r * HALO, HALO)
+        copy = send(box.at[block], inbox.at[block], in_s.at[r], in_r.at[r], beside(gx, gy, -dx, -dy))
+        copy.start()
+        arriving.append(copy)
+
     load_weights.wait()
     for m in range(NB):
         left = weights[2 * m]
@@ -147,14 +157,6 @@
         both = jnp.concatenate([high, turned - high], axis=1).astype(BF16)
         wback[m * 128 : m * 128 + 128, 0:128] = both
         wback[m * 128 : m * 128 + 128, 128:256] = both
-
-    pl.semaphore_wait(barrier, 8 + 1 + PLANE - 1 + DEEP - 1)
-    arriving = []
-    for r, (dx, dy) in enumerate(OFFSETS):
-        block = pl.ds(r * HALO, HALO)
-        copy = send(box.at[block], inbox.at[block], in_s.at[r], in_r.at[r], beside(gx, gy, -dx, -dy))
-        copy.start()
-        arriving.append(copy)
 
     def split_tile(t, carry):
         xh[t], xl[t] = halves(feat[t])
@@ -224,7 +226,7 @@
         for h in range(QUAD):
             tile = p * QUAD + h
             live = jnp.where(tile < counts[0, 0], 1.0, 0.0).astype(F32)
-            act[tile] = value[:, h * V : h * V + V] * live
+            feat[tile] = value[:, h * V : h * V + V] * live
             grads.append(cot[tile] * live * slope[:, h * V : h * V + V])
         gh, gl = halves(jnp.concatenate(grads, axis=1))
         stacked[p, 0:C] = gh
@@ -238,26 +240,37 @@
 
     lax.fori_loop(0, TILES // QUAD, forward, 0)
 
+    store_act = pltpu.make_async_copy(feat, act_hbm, store_sem.at[0])
+    store_act.start()
     core_copy = send(theirs, given, core_s, core_r, other)
 
-    def xy_copy(m, source, target):
-        return send(summed.at[m], xy_in.at[source], xy_s.at[m], xy_r.at[source], xy_device(target))
-
-    def z_copy(d, slot):
-        return send(z_in.at[slot], z_in.at[slot], z_s.at[d], z_r.at[slot], z_device(d))
-
-    def spread_copy(m, target):
-        return send(half.at[m], half.at[m], spread_s.at[target], spread_r.at[m], xy_device(target))
-
-    reducer = xy < NB
-    own = jnp.minimum(xy, NB - 1)
+    def fold_copy(d, target, source):
+        return send(summed.at[target], z_in.at[source], fold_s.at[d], fold_r.at[source], z_device(d))
+
+    def plane_copy(u, source):
+        return send(xy_in.at[source], xy_in.at[source], xy_s.at[u], xy_r.at[source], xy_device(u))
+
+    def spread_copy(d, source):
+        return send(half.at[source], half.at[source], spread_s.at[d], spread_r.at[source], z_device(d))
+
+    def others(act):
+        for u in range(PLANE):
+            pl.when(xy != u)(lambda u=u: act(u))
+
+    def tree(values):
+        while len(values) > 1:
+            values = [values[i] + values[i + 1] for i in range(0, len(values) - 1, 2)] + values[len(values) & ~1 :]
+        return values[0]
+
     for c in range(2):
 
         @pl.when(core == c)
         def _(c=c):
-            for m in range(NB):
-                mine[m] = total[c * 32 : c * 32 + 32, m * 128 : m * 128 + 128]
-                theirs[m] = total[32 - c * 32 : 64 - c * 32, m * 128 : m * 128 + 128]
+            for i in range(DEEP * PIECE // 8):
+                m, row = i // 4, (i % 4) * 8
+                mine[i // 7, (i % 7) * 8 : (i % 7) * 8 + 8] = total[c * 32 + row : c * 32 + row + 8, m * 128 : m * 128 + 128]
+                row += 32 - c * 32
+                theirs[i // 7, (i % 7) * 8 : (i % 7) * 8 + 8] = total[row : row + 8, m * 128 : m * 128 + 128]
 
     core_copy.start()
 
@@ -273,23 +286,16 @@
 
     lax.fori_loop(0, 2, backward, 0)
     core_copy.wait_recv()
-    for m in range(NB):
-        summed[m] = mine[m] + given[m]
-    for m in range(NB):
-        pl.when(xy != m)(lambda m=m: xy_copy(m, xy, m).start())
+    summed[...] = mine[...] + given[...]
+    for d in range(1, DEEP):
+        fold_copy(d, lax.rem(z + d, DEEP), z).start()
+    z_in[z] = summed[z]
     lax.fori_loop(2, TILES // QUAD, backward, 0)
 
-    @pl.when(reducer)
-    def _():
-        xy_in[xy] = summed[own]
-        for u in range(PLANE):
-            pl.when(xy != u)(lambda u=u: xy_copy(0, u, 0).wait_recv())
-        acc = xy_in[0]
-        for u in range(1, PLANE):
-            acc = acc + xy_in[u]
-        z_in[z] = acc
-        for d in range(1, DEEP):
-            z_copy(d, z).start()
+    for d in range(1, DEEP):
+        fold_copy(d, 0, lax.rem(z + d, DEEP)).wait_recv()
+    xy_in[xy] = tree([z_in[d] for d in range(DEEP)])
+    others(lambda u: plane_copy(u, xy).start())
 
     def scan(step, carry):
         acc, last = carry
@@ -319,54 +325,56 @@
         copy.start()
         leaving.append(copy)
 
-    @pl.when(reducer)
-    def _():
-        for d in range(1, DEEP):
-            z_copy(d, lax.rem(z + d, DEEP)).wait_recv()
-        acc = z_in[0]
-        for d in range(1, DEEP):
-            acc = acc + z_in[d]
-        half[own] = acc
-        for u in range(PLANE):
-            pl.when(xy != u)(lambda u=u: spread_copy(own, u).start())
-
     for t in range(TILES):
-        ge[t] = gathered(t)
-    for m in range(NB):
-        pl.when(xy != m)(lambda m=m: spread_copy(m, 0).wait_recv())
+        cot[t] = gathered(t)
+    store_ge = pltpu.make_async_copy(cot, ge_hbm, store_sem.at[1])
+    store_ge.start()
+    others(lambda u: plane_copy(u, u).wait_recv())
+    half[z] = tree([xy_in[u] for u in range(PLANE)])
+    for d in range(1, DEEP):
+        spread_copy(d, z).start()
+    for d in range(1, DEEP):
+        spread_copy(d, lax.rem(z + d, DEEP)).wait_recv()
     end = send(half, out.at[core], end_s, end_r, other)
     end.start()
-    out[core] = half[...]
+    store_half = pltpu.make_async_copy(half, out.at[core], store_sem.at[2])
+    store_half.start()
     core_copy.wait_send()
-    for m in range(NB):
-        pl.when(xy != m)(lambda m=m: xy_copy(m, xy, m).wait_send())
-
-    @pl.when(reducer)
-    def _():
-        for d in range(1, DEEP):
-            z_copy(d, z).wait_send()
-        for u in range(PLANE):
-            pl.when(xy != u)(lambda u=u: spread_copy(own, u).wait_send())
-
+    for d in range(1, DEEP):
+        fold_copy(d, 0, z).wait_send()
+        spread_copy(d, z).wait_send()
+    others(lambda u: plane_copy(u, xy).wait_send())
+    store_act.wait()
+    store_ge.wait()
+    store_half.wait()
     for copy in leaving:
         copy.wait()
     end.wait()
 
 
-def finish_kernel(sends, ge, back, summed, act, acts, gf, gwo):
+def finish_kernel(sends, ge_hbm, back_hbm, summed_hbm, act_hbm, acts_hbm, gf, gwo, back, summed, sem):
     gx, gy = position()
-    acts[...] = act[...]
-    gf[...] = ge[...]
+    load_sums = pltpu.make_async_copy(summed_hbm, summed, sem.at[0])
+    load_ge = pltpu.make_async_copy(ge_hbm, gf, sem.at[1])
+    load_back = pltpu.make_async_copy(back_hbm, back, sem.at[2])
+    move_act = pltpu.make_async_copy(act_hbm, acts_hbm, sem.at[3])
+    for copy in (load_sums, load_ge, load_back, move_act):
+        copy.start()
+    load_sums.wait()
+    for c in range(2):
+        for i in range(DEEP * PIECE // 8):
+            m, row = i // 4, c * 32 + (i % 4) * 8
+            block = summed[c, i // 7, (i % 7) * 8 : (i % 7) * 8 + 8]
+            gwo[2 * m, row : row + 8, :] = block[:, 0:C]
+            if 2 * m + 1 < OFFS:
+                gwo[2 * m + 1, row : row + 8, :] = block[:, C : 2 * C]
+    load_ge.wait()
+    load_back.wait()
     for r, (dx, dy) in enumerate(OFFSETS):
         there = inside(gx, gy, -dx, -dy)
         for h in range(HALO):
-            gf[sends[0, 0, r, h]] += back[r * HALO + h] * there
-    for c in range(2):
-        for m in range(NB):
-            block = summed[c, m]
-            gwo[2 * m, c * 32 : c * 32 + 32, :] = block[:, 0:C]
-            if 2 * m + 1 < OFFS:
-                gwo[2 * m + 1, c * 32 : c * 32 + 32, :] = block[:, C : 2 * C]
+            gf[sends[0, 0, h, r]] += back[r * HALO + h] * there
+    move_act.wait()
 
 
 def shaped(shape, dtype=F32):
@@ -374,6 +382,7 @@
 
 
 def per_device(features, weights, kernel_map, send_lists, counts, cotangent):
+    send_lists = jnp.swapaxes(send_lists, 2, 3)
     dma = pltpu.SemaphoreType.DMA
     vmem = pltpu.VMEM
     act, ge, back, summed = pl.pallas_call(
@@ -382,10 +391,10 @@
             shaped((TILES, C, V)),
             shaped((TILES, C, V)),
             shaped((8 * HALO, C, V)),
-            shaped((2, NB, 32, 128)),
+            shaped((2, DEEP, PIECE, 128)),
         ),
         in_specs=[SMEM, SMEM, SMEM, VMEM, ANY, ANY, ANY],
-        out_specs=(VMEM, VMEM, ANY, VMEM),
+        out_specs=(ANY, ANY, ANY, ANY),
         scratch_shapes=[
             vmem((TILES, C, V), F32),
             vmem((OFFS, C, C), F32),
@@ -406,13 +415,14 @@
             vmem((8, 128), jnp.int32),
             pltpu.SMEM((8, RANKS), jnp.int32),
             pltpu.SMEM((8, 128), jnp.int32),
-            vmem((NB, 32, 128), F32),
-            vmem((NB, 32, 128), F32),
-            vmem((NB, 32, 128), F32),
-            vmem((NB, 32, 128), F32),
-            vmem((PLANE, 32, 128), F32),
-            vmem((DEEP, 32, 128), F32),
-            vmem((NB, 32, 128), F32),
+            vmem((DEEP, PIECE, 128), F32),
+            vmem((DEEP, PIECE, 128), F32),
+            vmem((DEEP, PIECE, 128), F32),
+            vmem((DEEP, PIECE, 128), F32),
+            vmem((PLANE, PIECE, 128), F32),
+            vmem((DEEP, PIECE, 128), F32),
+            vmem((DEEP, PIECE, 128), F32),
+            dma((3,)),
             dma((3,)),
             dma((2,)),
             dma((8,)),
@@ -421,12 +431,12 @@
             dma((8,)),
             dma,
             dma,
-            dma((NB,)),
+            dma((PLANE,)),
             dma((PLANE,)),
             dma((DEEP,)),
             dma((DEEP,)),
-            dma((PLANE,)),
-            dma((NB,)),
+            dma((DEEP,)),
+            dma((DEEP,)),
             dma,
             dma,
         ],
@@ -435,9 +445,14 @@
     act, gf, gwo = pl.pallas_call(
         finish_kernel,
         out_shape=(shaped((TILES, C, V)), shaped((TILES, C, V)), shaped((OFFS, C, C))),
-        in_specs=[SMEM, VMEM, VMEM, VMEM, VMEM],
-        out_specs=(VMEM, VMEM, VMEM),
-        compiler_params=pltpu.CompilerParams(vmem_limit_bytes=24 << 20),
+        in_specs=[SMEM, ANY, ANY, ANY, ANY],
+        out_specs=(ANY, VMEM, VMEM),
+        scratch_shapes=[
+            vmem((8 * HALO, C, V), F32),
+            vmem((2, DEEP, PIECE, 128), F32),
+            dma((4,)),
+        ],
+        compiler_params=pltpu.CompilerParams(vmem_limit_bytes=60 << 20),
     )(send_lists, ge, back, summed, act)
     return act[None, None], gf[None, None], gwo
 

time: 81.6 us -> 103 us (1.26)
  Pallas kernels: 73.4 us -> 101 us
  local copies, waits for them, and re-layouts: 6.54 us -> 0 us
    pallas_call x1, Pallas kernels: 2.31 us -> 26.8 us  [per_device(): pl.pallas_call(finish_kernel, out_shape=(shaped((TILES, C, V)), shaped((T...]
    unnamed x11 -> x0, local copies, waits for them, and re-layouts: 6.54 us -> none
    pallas_call x1, Pallas kernels: 71.1 us -> 74.1 us  [per_device(): pl.pallas_call(main_kernel, out_shape=(shaped((TILES, C, V)), shaped((TIL...]
where the time goes in v4:
time: 103 us; the launch traced here: 102 us
  Pallas kernels  101 us (98%)
  between operations  1.29 us (1%)
    pallas_call x1, Pallas kernels, per_device(): pl.pallas_call(main_kernel, out_shape=(shaped((TILES, C, V)), shaped((TIL...  74.1 us
    pallas_call x1, Pallas kernels, per_device(): pl.pallas_call(finish_kernel, out_shape=(shaped((TILES, C, V)), shaped((T...  26.8 us

profile of v4, /device:TPU:1, one launch (start us, length us, event | category | flops | bytes accessed | tf_op | source)
XLA Modules:
  0.0 102.2 jit_solution(9939056787207476975)
XLA Ops:
  1.3 74.1 %shard_map.85 = (f32[24,64,128]{2,1,0:T(8,128)}, f32[24,64,128]{2,1,0:T(8,128)}, f32[32,64,128]{2,1,0:T(8,128)}, f32[2,8,56,128]{3,2,1,0:T(8,128)}) custom-call(s32[1,1,24,27]{3,2,1,0:T(8,128)} %kmap_rows.1, s32[1,1,4,8]{3,2,1,0:T(4,128)} %bitcast.3, s32[1,1]{1,0:T(1,128)S(6)} %copy.9.counts, s32[1,1,24,27]{3,2,1,0:T(8,128)} %kmap_rows.1, ...), custom_call_target="tpu_custom_call" | custom-call | tf_op jit(solution)/shard_map/pallas_call | solution.py:388
  75.4 26.8 %shard_map.86 = (f32[24,64,128]{2,1,0:T(8,128)}, f32[24,64,128]{2,1,0:T(8,128)}, f32[27,64,64]{2,1,0:T(8,128)}) custom-call(s32[1,1,4,8]{3,2,1,0:T(4,128)} %bitcast.4, f32[24,64,128]{2,1,0:T(8,128)} %get-tuple-element.10.ge_hbm, f32[32,64,128]{2,1,0:T(8,128)} %get-tuple-element.11.back_hbm, f32[2,8,56,128]{3,2,1,0:T(8,128)} %get-tuple-element.12.summed_hbm, ...), custom_call_target="tpu_custom_call" | custom-call | tf_op jit(solution)/shard_map/pallas_call | solution.py:445

commit v5 on v4

--- a/solution.py
+++ b/solution.py
@@ -13,9 +13,10 @@
 NB = KC // 128
 PLANE, DEEP = 16, 8
 QUAD = 4
+EARLY = (0, 2, 5, 7)
+LATE = (1, 3, 4, 6)
 ENTRIES = TILES * OFFS
 RANKS = 768
-PIECE = 56
 MESH = pl.DeviceIdType.MESH
 F32, BF16 = jnp.float32, jnp.bfloat16
 VMEM = pl.BlockSpec(memory_space=pltpu.VMEM)
@@ -64,6 +65,8 @@
     inbox,
     catch,
     catl,
+    nexth,
+    nextl,
     total,
     stacked,
     parts,
@@ -166,8 +169,8 @@
     xh[WIDE - 1] = jnp.zeros((C, V), BF16)
     xl[WIDE - 1] = jnp.zeros((C, V), BF16)
     total[...] = jnp.zeros_like(total)
-    catch[OFFS * C : KC, :] = jnp.zeros((C, QUAD * V), BF16)
-    catl[OFFS * C : KC, :] = jnp.zeros((C, QUAD * V), BF16)
+    for panel in (catch, catl, nexth, nextl):
+        panel[OFFS * C : KC, :] = jnp.zeros((C, 2 * V), BF16)
 
     place = lax.broadcasted_iota(jnp.int32, (TILES, OFFS), 0) * OFFS + lax.broadcasted_iota(jnp.int32, (TILES, OFFS), 1)
     keys = kmap_rows[0, 0] * 1024 + place
@@ -210,48 +213,75 @@
 
     contract_last = (((1,), (1,)), ((), ()))
 
-    def forward(p, carry):
+    even, odd = (catch, catl), (nexth, nextl)
+    pairs = TILES // 2
+
+    def fill(p, panels):
         for k in range(OFFS):
-            for h in range(QUAD):
-                slot = kmap[0, 0, p * QUAD + h, k]
-                catch[k * C : k * C + C, h * V : h * V + V] = xh[slot]
-                catl[k * C : k * C + C, h * V : h * V + V] = xl[slot]
-        first = jnp.dot(wcat[...], catch[...], preferred_element_type=F32)
-        second = jnp.dot(wcat[0:C, :], catl[...], preferred_element_type=F32)
-        pre = first[0:C] + first[C:] + second
+            for h in range(2):
+                slot = kmap[0, 0, p * 2 + h, k]
+                panels[0][k * C : k * C + C, h * V : h * V + V] = xh[slot]
+                panels[1][k * C : k * C + C, h * V : h * V + V] = xl[slot]
+
+    def product(panels):
+        first = jnp.dot(wcat[...], panels[0][...], preferred_element_type=F32)
+        second = jnp.dot(wcat[0:C, :], panels[1][...], preferred_element_type=F32)
+        return first[0:C] + first[C:] + second
+
+    def activate(p, pre):
         sig = jax.nn.sigmoid(pre)
         slope = sig * (1.0 + pre * (1.0 - sig))
         value = pre * sig
         grads = []
-        for h in range(QUAD):
-            tile = p * QUAD + h
+        for h in range(2):
+            tile = p * 2 + h
             live = jnp.where(tile < counts[0, 0], 1.0, 0.0).astype(F32)
             feat[tile] = value[:, h * V : h * V + V] * live
             grads.append(cot[tile] * live * slope[:, h * V : h * V + V])
         gh, gl = halves(jnp.concatenate(grads, axis=1))
         stacked[p, 0:C] = gh
         stacked[p, C : 2 * C] = gl
-        two = lax.dot_general(
-            jnp.concatenate([gh, gl], axis=0), catch[...], contract_last, preferred_element_type=F32
-        )
-        one = lax.dot_general(gh, catl[...], contract_last, preferred_element_type=F32)
+
+    def weigh(p, panels):
+        two = lax.dot_general(stacked[p], panels[0][...], contract_last, preferred_element_type=F32)
+        one = lax.dot_general(stacked[p, 0:C], panels[1][...], contract_last, preferred_element_type=F32)
         total[...] += two[0:C] + two[C:] + one
+
+    def advance(p, panels, last):
+        fill(p, panels)
+        pre = product(panels)
+        weigh(p - 1, last)
+        activate(p, pre)
+
+    def two_pairs(i, carry):
+        advance(2 * i + 1, odd, even)
+        advance(2 * i + 2, even, odd)
         return carry
 
-    lax.fori_loop(0, TILES // QUAD, forward, 0)
-
+    fill(0, even)
+    activate(0, product(even))
+    lax.fori_loop(0, pairs // 2 - 1, two_pairs, 0)
+    advance(pairs - 1, odd, even)
+    weigh(pairs - 1, odd)
     store_act = pltpu.make_async_copy(feat, act_hbm, store_sem.at[0])
     store_act.start()
     core_copy = send(theirs, given, core_s, core_r, other)
 
-    def fold_copy(d, target, source):
-        return send(summed.at[target], z_in.at[source], fold_s.at[d], fold_r.at[source], z_device(d))
-
-    def plane_copy(u, source):
-        return send(xy_in.at[source], xy_in.at[source], xy_s.at[u], xy_r.at[source], xy_device(u))
-
-    def spread_copy(d, source):
-        return send(half.at[source], half.at[source], spread_s.at[d], spread_r.at[source], z_device(d))
+    def fold_copy(m, source):
+        return send(summed.at[m], xy_in.at[source], xy_s.at[m], xy_r.at[source], xy_device(m))
+
+    def z_copy(d, source):
+        return send(z_in.at[source], z_in.at[source], fold_s.at[d], fold_r.at[source], z_device(d))
+
+    def spread_copy(u, m):
+        return send(half.at[m], half.at[m], spread_s.at[u], spread_r.at[m], xy_device(u))
+
+    reducer = xy < NB
+    own = jnp.minimum(xy, NB - 1)
+
+    def pieces(act):
+        for m in range(NB):
+            pl.when(xy != m)(lambda m=m: act(m))
 
     def others(act):
         for u in range(PLANE):
@@ -266,17 +296,15 @@
 
         @pl.when(core == c)
         def _(c=c):
-            for i in range(DEEP * PIECE // 8):
-                m, row = i // 4, (i % 4) * 8
-                mine[i // 7, (i % 7) * 8 : (i % 7) * 8 + 8] = total[c * 32 + row : c * 32 + row + 8, m * 128 : m * 128 + 128]
-                row += 32 - c * 32
-                theirs[i // 7, (i % 7) * 8 : (i % 7) * 8 + 8] = total[row : row + 8, m * 128 : m * 128 + 128]
+            for m in range(NB):
+                mine[m] = total[c * 32 : c * 32 + 32, m * 128 : m * 128 + 128]
+                theirs[m] = total[32 - c * 32 : 64 - c * 32, m * 128 : m * 128 + 128]
 
     core_copy.start()
 
     def backward(p, carry):
-        gh = stacked[p, 0:C]
-        gl = stacked[p, C : 2 * C]
+        gh = jnp.concatenate([stacked[2 * p, 0:C], stacked[2 * p + 1, 0:C]], axis=1)
+        gl = jnp.concatenate([stacked[2 * p, C : 2 * C], stacked[2 * p + 1, C : 2 * C]], axis=1)
         four = jnp.concatenate([gh, gh, gl, gl], axis=0)
         for k in range(OFFS):
             part = jnp.dot(wback[k * C : k * C + C, :], four, preferred_element_type=F32)
@@ -287,15 +315,16 @@
     lax.fori_loop(0, 2, backward, 0)
     core_copy.wait_recv()
     summed[...] = mine[...] + given[...]
-    for d in range(1, DEEP):
-        fold_copy(d, lax.rem(z + d, DEEP), z).start()
-    z_in[z] = summed[z]
+    pieces(lambda m: fold_copy(m, xy).start())
+    xy_in[xy] = summed[own]
     lax.fori_loop(2, TILES // QUAD, backward, 0)
 
-    for d in range(1, DEEP):
-        fold_copy(d, 0, lax.rem(z + d, DEEP)).wait_recv()
-    xy_in[xy] = tree([z_in[d] for d in range(DEEP)])
-    others(lambda u: plane_copy(u, xy).start())
+    @pl.when(reducer)
+    def _():
+        others(lambda u: fold_copy(0, u).wait_recv())
+        z_in[z] = tree([xy_in[u] for u in range(PLANE)])
+        for d in range(1, DEEP):
+            z_copy(d, z).start()
 
     def scan(step, carry):
         acc, last = carry
@@ -317,7 +346,8 @@
         return runs[jnp.maximum(stop - 1, 0)] * jnp.where(stop > begin, 1.0, 0.0).astype(F32)
 
     leaving = []
-    for r, (dx, dy) in enumerate(OFFSETS):
+
+    def leave(r, dx, dy):
         for h in range(HALO):
             box[r * HALO + h] = gathered(TILES + r * HALO + h)
         block = pl.ds(r * HALO, HALO)
@@ -325,25 +355,36 @@
         copy.start()
         leaving.append(copy)
 
+    for r in EARLY:
+        leave(r, *OFFSETS[r])
+
+    @pl.when(reducer)
+    def _():
+        for d in range(1, DEEP):
+            z_copy(d, lax.rem(z + d, DEEP)).wait_recv()
+        half[own] = tree([z_in[d] for d in range(DEEP)])
+        others(lambda u: spread_copy(u, own).start())
+
+    for r in LATE:
+        leave(r, *OFFSETS[r])
     for t in range(TILES):
         cot[t] = gathered(t)
     store_ge = pltpu.make_async_copy(cot, ge_hbm, store_sem.at[1])
     store_ge.start()
-    others(lambda u: plane_copy(u, u).wait_recv())
-    half[z] = tree([xy_in[u] for u in range(PLANE)])
-    for d in range(1, DEEP):
-        spread_copy(d, z).start()
-    for d in range(1, DEEP):
-        spread_copy(d, lax.rem(z + d, DEEP)).wait_recv()
+    pieces(lambda m: spread_copy(0, m).wait_recv())
     end = send(half, out.at[core], end_s, end_r, other)
     end.start()
     store_half = pltpu.make_async_copy(half, out.at[core], store_sem.at[2])
     store_half.start()
     core_copy.wait_send()
-    for d in range(1, DEEP):
-        fold_copy(d, 0, z).wait_send()
-        spread_copy(d, z).wait_send()
-    others(lambda u: plane_copy(u, xy).wait_send())
+    pieces(lambda m: fold_copy(m, xy).wait_send())
+
+    @pl.when(reducer)
+    def _():
+        for d in range(1, DEEP):
+            z_copy(d, z).wait_send()
+        others(lambda u: spread_copy(u, own).wait_send())
+
     store_act.wait()
     store_ge.wait()
     store_half.wait()
@@ -352,22 +393,21 @@
     end.wait()
 
 
-def finish_kernel(sends, ge_hbm, back_hbm, summed_hbm, act_hbm, acts_hbm, gf, gwo, back, summed, sem):
+def finish_kernel(sends, ge_hbm, back_hbm, summed_hbm, act_hbm, acts, gf, gwo, back, summed, sem):
     gx, gy = position()
     load_sums = pltpu.make_async_copy(summed_hbm, summed, sem.at[0])
     load_ge = pltpu.make_async_copy(ge_hbm, gf, sem.at[1])
     load_back = pltpu.make_async_copy(back_hbm, back, sem.at[2])
-    move_act = pltpu.make_async_copy(act_hbm, acts_hbm, sem.at[3])
+    move_act = pltpu.make_async_copy(act_hbm, acts, sem.at[3])
     for copy in (load_sums, load_ge, load_back, move_act):
         copy.start()
     load_sums.wait()
     for c in range(2):
-        for i in range(DEEP * PIECE // 8):
-            m, row = i // 4, c * 32 + (i % 4) * 8
-            block = summed[c, i // 7, (i % 7) * 8 : (i % 7) * 8 + 8]
-            gwo[2 * m, row : row + 8, :] = block[:, 0:C]
+        for m in range(NB):
+            block = summed[c, m]
+            gwo[2 * m, c * 32 : c * 32 + 32, :] = block[:, 0:C]
             if 2 * m + 1 < OFFS:
-                gwo[2 * m + 1, row : row + 8, :] = block[:, C : 2 * C]
+                gwo[2 * m + 1, c * 32 : c * 32 + 32, :] = block[:, C : 2 * C]
     load_ge.wait()
     load_back.wait()
     for r, (dx, dy) in enumerate(OFFSETS):
@@ -391,7 +431,7 @@
             shaped((TILES, C, V)),
             shaped((TILES, C, V)),
             shaped((8 * HALO, C, V)),
-            shaped((2, DEEP, PIECE, 128)),
+            shaped((2, NB, 32, 128)),
         ),
         in_specs=[SMEM, SMEM, SMEM, VMEM, ANY, ANY, ANY],
         out_specs=(ANY, ANY, ANY, ANY),
@@ -405,23 +445,25 @@
             vmem((KC, 4 * C), BF16),
             vmem((8 * HALO, C, V), F32),
             vmem((8 * HALO, C, V), F32),
-            vmem((KC, QUAD * V), BF16),
-            vmem((KC, QUAD * V), BF16),
+            vmem((KC, 2 * V), BF16),
+            vmem((KC, 2 * V), BF16),
+            vmem((KC, 2 * V), BF16),
+            vmem((KC, 2 * V), BF16),
             vmem((C, KC), F32),
-            vmem((TILES // QUAD, 2 * C, QUAD * V), BF16),
+            vmem((TILES // 2, 2 * C, 2 * V), BF16),
             vmem((ENTRIES, C, V), F32),
             vmem((ENTRIES, C, V), F32),
             vmem((8, RANKS), jnp.int32),
             vmem((8, 128), jnp.int32),
             pltpu.SMEM((8, RANKS), jnp.int32),
             pltpu.SMEM((8, 128), jnp.int32),
-            vmem((DEEP, PIECE, 128), F32),
-            vmem((DEEP, PIECE, 128), F32),
-            vmem((DEEP, PIECE, 128), F32),
-            vmem((DEEP, PIECE, 128), F32),
-            vmem((PLANE, PIECE, 128), F32),
-            vmem((DEEP, PIECE, 128), F32),
-            vmem((DEEP, PIECE, 128), F32),
+            vmem((NB, 32, 128), F32),
+            vmem((NB, 32, 128), F32),
+            vmem((NB, 32, 128), F32),
+            vmem((NB, 32, 128), F32),
+            vmem((PLANE, 32, 128), F32),
+            vmem((DEEP, 32, 128), F32),
+            vmem((NB, 32, 128), F32),
             dma((3,)),
             dma((3,)),
             dma((2,)),
@@ -431,12 +473,12 @@
             dma((8,)),
             dma,
             dma,
-            dma((PLANE,)),
+            dma((NB,)),
             dma((PLANE,)),
             dma((DEEP,)),
             dma((DEEP,)),
-            dma((DEEP,)),
-            dma((DEEP,)),
+            dma((PLANE,)),
+            dma((NB,)),
             dma,
             dma,
         ],
@@ -446,10 +488,10 @@
         finish_kernel,
         out_shape=(shaped((TILES, C, V)), shaped((TILES, C, V)), shaped((OFFS, C, C))),
         in_specs=[SMEM, ANY, ANY, ANY, ANY],
-        out_specs=(ANY, VMEM, VMEM),
+        out_specs=(VMEM, VMEM, VMEM),
         scratch_shapes=[
             vmem((8 * HALO, C, V), F32),
-            vmem((2, DEEP, PIECE, 128), F32),
+            vmem((2, NB, 32, 128), F32),
             dma((4,)),
         ],
         compiler_params=pltpu.CompilerParams(vmem_limit_bytes=60 << 20),

time: 103 us -> 73.9 us (0.72)
  Pallas kernels: 101 us -> 72.4 us
    pallas_call x1, Pallas kernels: 26.8 us -> 3.98 us  [per_device(): pl.pallas_call(finish_kernel, out_shape=(shaped((TILES, C, V)), shaped((T...]
    pallas_call x1, Pallas kernels: 74.1 us -> 68.4 us  [per_device(): pl.pallas_call(main_kernel, out_shape=(shaped((TILES, C, V)), shaped((TIL...]
where the time goes in v5:
time: 73.9 us; the launch traced here: 73.6 us
  Pallas kernels  72.4 us (98%)
  between operations  1.29 us (2%)
    pallas_call x1, Pallas kernels, per_device(): pl.pallas_call(main_kernel, out_shape=(shaped((TILES, C, V)), shaped((TIL...  68.4 us
    pallas_call x1, Pallas kernels, per_device(): pl.pallas_call(finish_kernel, out_shape=(shaped((TILES, C, V)), shaped((T...  3.98 us

profile of v5, /device:TPU:1, one launch (start us, length us, event | category | flops | bytes accessed | tf_op | source)
XLA Modules:
  0.0 73.6 jit_solution(12398822770699392140)
XLA Ops:
  1.3 68.4 %shard_map.85 = (f32[24,64,128]{2,1,0:T(8,128)}, f32[24,64,128]{2,1,0:T(8,128)}, f32[32,64,128]{2,1,0:T(8,128)}, f32[2,14,32,128]{3,2,1,0:T(8,128)}) custom-call(s32[1,1,24,27]{3,2,1,0:T(8,128)} %kmap_rows.1, s32[1,1,4,8]{3,2,1,0:T(4,128)} %bitcast.3, s32[1,1]{1,0:T(1,128)S(6)} %copy.9.counts, s32[1,1,24,27]{3,2,1,0:T(8,128)} %kmap_rows.1, ...), custom_call_target="tpu_custom_call" | custom-call | tf_op jit(solution)/shard_map/pallas_call | solution.py:428
  69.7 4.0 %shard_map.86 = (f32[24,64,128]{2,1,0:T(8,128)}, f32[24,64,128]{2,1,0:T(8,128)}, f32[27,64,64]{2,1,0:T(8,128)}) custom-call(s32[1,1,4,8]{3,2,1,0:T(4,128)} %bitcast.4, f32[24,64,128]{2,1,0:T(8,128)} %get-tuple-element.10.ge_hbm, f32[32,64,128]{2,1,0:T(8,128)} %get-tuple-element.11.back_hbm, f32[2,14,32,128]{3,2,1,0:T(8,128)} %get-tuple-element.12.summed_hbm, ...), custom_call_target="tpu_custom_call" | custom-call | tf_op jit(solution)/shard_map/pallas_call | solution.py:487

commit v6 on v5

--- a/solution.py
+++ b/solution.py
@@ -13,8 +13,9 @@
 NB = KC // 128
 PLANE, DEEP = 16, 8
 QUAD = 4
+HALFWAY = 40
 EARLY = (0, 2, 5, 7)
-LATE = (1, 3, 4, 6)
+LATE = (3, 4, 1, 6)
 ENTRIES = TILES * OFFS
 RANKS = 768
 MESH = pl.DeviceIdType.MESH
@@ -125,10 +126,10 @@
     for d in range(1, DEEP):
         greet(z_device(d))
     for dx, dy in OFFSETS:
-        greet(beside(gx, gy, dx, dy))
+        if dx != 0:
+            greet(beside(gx, gy, dx, dy))
     for u in range(PLANE):
         pl.when(xy != u)(lambda u=u: greet(xy_device(u)))
-    greet(other)
 
     def send(src, dst, send_sem, recv_sem, device):
         return pltpu.make_async_remote_copy(
@@ -139,7 +140,7 @@
     for r in range(8):
         for h in range(HALO):
             box[r * HALO + h] = feat[sends[0, 0, h, r]]
-    pl.semaphore_wait(barrier, 8 + 1 + PLANE - 1 + DEEP - 1)
+    pl.semaphore_wait(barrier, 6 + PLANE - 1 + DEEP - 1)
     arriving = []
     for r, (dx, dy) in enumerate(OFFSETS):
         block = pl.ds(r * HALO, HALO)
@@ -319,13 +320,6 @@
     xy_in[xy] = summed[own]
     lax.fori_loop(2, TILES // QUAD, backward, 0)
 
-    @pl.when(reducer)
-    def _():
-        others(lambda u: fold_copy(0, u).wait_recv())
-        z_in[z] = tree([xy_in[u] for u in range(PLANE)])
-        for d in range(1, DEEP):
-            z_copy(d, z).start()
-
     def scan(step, carry):
         acc, last = carry
         for i in range(8):
@@ -338,7 +332,16 @@
             last = entry
         return acc, last
 
-    lax.fori_loop(0, ENTRIES // 8, scan, (jnp.zeros((C, V), F32), jnp.int32(WIDE)))
+    midway = lax.fori_loop(0, HALFWAY, scan, (jnp.zeros((C, V), F32), jnp.int32(WIDE)))
+
+    @pl.when(reducer)
+    def _():
+        others(lambda u: fold_copy(0, u).wait_recv())
+        z_in[z] = tree([xy_in[u] for u in range(PLANE)])
+        for d in range(1, DEEP):
+            z_copy(d, z).start()
+
+    lax.fori_loop(HALFWAY, ENTRIES // 8, scan, midway)
 
     def gathered(entry):
         stop = upto[0, entry]
@@ -393,13 +396,16 @@
     end.wait()
 
 
-def finish_kernel(sends, ge_hbm, back_hbm, summed_hbm, act_hbm, acts, gf, gwo, back, summed, sem):
+def finish_kernel(sends, ge_hbm, back_hbm, summed_hbm, act_hbm, acts_hbm, gf_hbm, gwo_hbm, acts, gf, gwo, back, summed, sem):
     gx, gy = position()
     load_sums = pltpu.make_async_copy(summed_hbm, summed, sem.at[0])
     load_ge = pltpu.make_async_copy(ge_hbm, gf, sem.at[1])
     load_back = pltpu.make_async_copy(back_hbm, back, sem.at[2])
-    move_act = pltpu.make_async_copy(act_hbm, acts, sem.at[3])
-    for copy in (load_sums, load_ge, load_back, move_act):
+    load_act = pltpu.make_async_copy(act_hbm, acts, sem.at[3])
+    store_act = pltpu.make_async_copy(acts, acts_hbm, sem.at[4])
+    store_gwo = pltpu.make_async_copy(gwo, gwo_hbm, sem.at[5])
+    store_gf = pltpu.make_async_copy(gf, gf_hbm, sem.at[6])
+    for copy in (load_sums, load_act, load_ge, load_back):
         copy.start()
     load_sums.wait()
     for c in range(2):
@@ -408,13 +414,19 @@
             gwo[2 * m, c * 32 : c * 32 + 32, :] = block[:, 0:C]
             if 2 * m + 1 < OFFS:
                 gwo[2 * m + 1, c * 32 : c * 32 + 32, :] = block[:, C : 2 * C]
+    store_gwo.start()
+    load_act.wait()
+    store_act.start()
     load_ge.wait()
     load_back.wait()
     for r, (dx, dy) in enumerate(OFFSETS):
         there = inside(gx, gy, -dx, -dy)
         for h in range(HALO):
             gf[sends[0, 0, h, r]] += back[r * HALO + h] * there
-    move_act.wait()
+    store_gf.start()
+    store_act.wait()
+    store_gwo.wait()
+    store_gf.wait()
 
 
 def shaped(shape, dtype=F32):
@@ -488,11 +500,14 @@
         finish_kernel,
         out_shape=(shaped((TILES, C, V)), shaped((TILES, C, V)), shaped((OFFS, C, C))),
         in_specs=[SMEM, ANY, ANY, ANY, ANY],
-        out_specs=(VMEM, VMEM, VMEM),
+        out_specs=(ANY, ANY, ANY),
         scratch_shapes=[
+            vmem((TILES, C, V), F32),
+            vmem((TILES, C, V), F32),
+            vmem((OFFS, C, C), F32),
             vmem((8 * HALO, C, V), F32),
             vmem((2, NB, 32, 128), F32),
-            dma((4,)),
+            dma((7,)),
         ],
         compiler_params=pltpu.CompilerParams(vmem_limit_bytes=60 << 20),
     )(send_lists, ge, back, summed, act)

time: 73.9 us -> 71.9 us (0.973)
  Pallas kernels: 72.4 us -> 70.4 us
    pallas_call x1, Pallas kernels: 68.4 us -> 66.7 us  [per_device(): pl.pallas_call(main_kernel, out_shape=(shaped((TILES, C, V)), shaped((TIL...]
where the time goes in v6:
time: 71.9 us; the launch traced here: 71.6 us
  Pallas kernels  70.4 us (98%)
  between operations  1.29 us (2%)
    pallas_call x1, Pallas kernels, per_device(): pl.pallas_call(main_kernel, out_shape=(shaped((TILES, C, V)), shaped((TIL...  66.7 us
    pallas_call x1, Pallas kernels, per_device(): pl.pallas_call(finish_kernel, out_shape=(shaped((TILES, C, V)), shaped((T...  3.64 us

profile of v6, /device:TPU:1, one launch (start us, length us, event | category | flops | bytes accessed | tf_op | source)
XLA Modules:
  0.0 71.6 jit_solution(17370142299153115639)
XLA Ops:
  1.3 66.7 %shard_map.85 = (f32[24,64,128]{2,1,0:T(8,128)}, f32[24,64,128]{2,1,0:T(8,128)}, f32[32,64,128]{2,1,0:T(8,128)}, f32[2,14,32,128]{3,2,1,0:T(8,128)}) custom-call(s32[1,1,24,27]{3,2,1,0:T(8,128)} %kmap_rows.1, s32[1,1,4,8]{3,2,1,0:T(4,128)} %bitcast.3, s32[1,1]{1,0:T(1,128)S(6)} %copy.9.counts, s32[1,1,24,27]{3,2,1,0:T(8,128)} %kmap_rows.1, ...), custom_call_target="tpu_custom_call" | custom-call | tf_op jit(solution)/shard_map/pallas_call | solution.py:440
  68.0 3.6 %shard_map.86 = (f32[24,64,128]{2,1,0:T(8,128)}, f32[24,64,128]{2,1,0:T(8,128)}, f32[27,64,64]{2,1,0:T(8,128)}) custom-call(s32[1,1,4,8]{3,2,1,0:T(4,128)} %bitcast.4, f32[24,64,128]{2,1,0:T(8,128)} %get-tuple-element.10.ge_hbm, f32[32,64,128]{2,1,0:T(8,128)} %get-tuple-element.11.back_hbm, f32[2,14,32,128]{3,2,1,0:T(8,128)} %get-tuple-element.12.summed_hbm, ...), custom_call_target="tpu_custom_call" | custom-call | tf_op jit(solution)/shard_map/pallas_call | solution.py:499

commit v7 on v6

--- a/solution.py
+++ b/solution.py
@@ -13,7 +13,16 @@
 NB = KC // 128
 PLANE, DEEP = 16, 8
 QUAD = 4
+
+
+def hops(step):
+    return min(step, 4 - step)
+
+
+FAR_FIRST = sorted([(a, b) for a in range(4) for b in range(4) if a or b], key=lambda s: -hops(s[0]) - hops(s[1]))
+DEPTHS = (4, 3, 5, 2, 6, 1, 7)
 HALFWAY = 40
+BEFORE = 2
 EARLY = (0, 2, 5, 7)
 LATE = (3, 4, 1, 6)
 ENTRIES = TILES * OFFS
@@ -281,12 +290,17 @@
     own = jnp.minimum(xy, NB - 1)
 
     def pieces(act):
-        for m in range(NB):
-            pl.when(xy != m)(lambda m=m: act(m))
+        for m in members():
+            pl.when(m < NB)(lambda m=m: act(m))
+
+    row, column = xy // 4, lax.rem(xy, 4)
+
+    def members():
+        return [lax.rem(row + a, 4) * 4 + lax.rem(column + b, 4) for a, b in FAR_FIRST]
 
     def others(act):
-        for u in range(PLANE):
-            pl.when(xy != u)(lambda u=u: act(u))
+        for u in members():
+            act(u)
 
     def tree(values):
         while len(values) > 1:
@@ -313,12 +327,12 @@
                 parts[(p * QUAD + h) * OFFS + k] = part[:, h * V : h * V + V]
         return carry
 
-    lax.fori_loop(0, 2, backward, 0)
+    lax.fori_loop(0, BEFORE, backward, 0)
     core_copy.wait_recv()
     summed[...] = mine[...] + given[...]
     pieces(lambda m: fold_copy(m, xy).start())
     xy_in[xy] = summed[own]
-    lax.fori_loop(2, TILES // QUAD, backward, 0)
+    lax.fori_loop(BEFORE, TILES // QUAD, backward, 0)
 
     def scan(step, carry):
         acc, last = carry
@@ -338,7 +352,7 @@
     def _():
         others(lambda u: fold_copy(0, u).wait_recv())
         z_in[z] = tree([xy_in[u] for u in range(PLANE)])
-        for d in range(1, DEEP):
+        for d in DEPTHS:
             z_copy(d, z).start()
 
     lax.fori_loop(HALFWAY, ENTRIES // 8, scan, midway)

time: 71.9 us -> 72.2 us (level)
  no operation moved by 1% of the time
where the time goes in v7:
time: 72.2 us; the launch traced here: 72 us
  Pallas kernels  70.7 us (98%)
  between operations  1.29 us (2%)
    pallas_call x1, Pallas kernels, per_device(): pl.pallas_call(main_kernel, out_shape=(shaped((TILES, C, V)), shaped((TIL...  67.1 us
    pallas_call x1, Pallas kernels, per_device(): pl.pallas_call(finish_kernel, out_shape=(shaped((TILES, C, V)), shaped((T...  3.64 us

profile of v7, /device:TPU:1, one launch (start us, length us, event | category | flops | bytes accessed | tf_op | source)
XLA Modules:
  0.0 72.0 jit_solution(2114440720353759437)
XLA Ops:
  1.3 67.1 %shard_map.85 = (f32[24,64,128]{2,1,0:T(8,128)}, f32[24,64,128]{2,1,0:T(8,128)}, f32[32,64,128]{2,1,0:T(8,128)}, f32[2,14,32,128]{3,2,1,0:T(8,128)}) custom-call(s32[1,1,24,27]{3,2,1,0:T(8,128)} %kmap_rows.1, s32[1,1,4,8]{3,2,1,0:T(4,128)} %bitcast.3, s32[1,1]{1,0:T(1,128)S(6)} %copy.9.counts, s32[1,1,24,27]{3,2,1,0:T(8,128)} %kmap_rows.1, ...), custom_call_target="tpu_custom_call" | custom-call | tf_op jit(solution)/shard_map/pallas_call | solution.py:454
  68.3 3.6 %shard_map.86 = (f32[24,64,128]{2,1,0:T(8,128)}, f32[24,64,128]{2,1,0:T(8,128)}, f32[27,64,64]{2,1,0:T(8,128)}) custom-call(s32[1,1,4,8]{3,2,1,0:T(4,128)} %bitcast.4, f32[24,64,128]{2,1,0:T(8,128)} %get-tuple-element.10.ge_hbm, f32[32,64,128]{2,1,0:T(8,128)} %get-tuple-element.11.back_hbm, f32[2,14,32,128]{3,2,1,0:T(8,128)} %get-tuple-element.12.summed_hbm, ...), custom_call_target="tpu_custom_call" | custom-call | tf_op jit(solution)/shard_map/pallas_call | solution.py:513

commit v8 on v6

--- a/solution.py
+++ b/solution.py
@@ -405,8 +405,17 @@
     store_act = pltpu.make_async_copy(acts, acts_hbm, sem.at[4])
     store_gwo = pltpu.make_async_copy(gwo, gwo_hbm, sem.at[5])
     store_gf = pltpu.make_async_copy(gf, gf_hbm, sem.at[6])
-    for copy in (load_sums, load_act, load_ge, load_back):
+    for copy in (load_ge, load_back, load_sums, load_act):
         copy.start()
+    load_ge.wait()
+    load_back.wait()
+    for r, (dx, dy) in enumerate(OFFSETS):
+        there = inside(gx, gy, -dx, -dy)
+        for h in range(HALO):
+            gf[sends[0, 0, h, r]] += back[r * HALO + h] * there
+    store_gf.start()
+    load_act.wait()
+    store_act.start()
     load_sums.wait()
     for c in range(2):
         for m in range(NB):
@@ -415,15 +424,6 @@
             if 2 * m + 1 < OFFS:
                 gwo[2 * m + 1, c * 32 : c * 32 + 32, :] = block[:, C : 2 * C]
     store_gwo.start()
-    load_act.wait()
-    store_act.start()
-    load_ge.wait()
-    load_back.wait()
-    for r, (dx, dy) in enumerate(OFFSETS):
-        there = inside(gx, gy, -dx, -dy)
-        for h in range(HALO):
-            gf[sends[0, 0, h, r]] += back[r * HALO + h] * there
-    store_gf.start()
     store_act.wait()
     store_gwo.wait()
     store_gf.wait()

time: 71.9 us -> 72.1 us (level)
  no operation moved by 1% of the time
where the time goes in v8:
time: 72.1 us; the launch traced here: 71.8 us
  Pallas kernels  70.5 us (98%)
  between operations  1.29 us (2%)
    pallas_call x1, Pallas kernels, per_device(): pl.pallas_call(main_kernel, out_shape=(shaped((TILES, C, V)), shaped((TIL...  66.7 us
    pallas_call x1, Pallas kernels, per_device(): pl.pallas_call(finish_kernel, out_shape=(shaped((TILES, C, V)), shaped((T...  3.81 us

profile of v8, /device:TPU:1, one launch (start us, length us, event | category | flops | bytes accessed | tf_op | source)
XLA Modules:
  0.0 71.8 jit_solution(18129883894503841540)
XLA Ops:
  1.3 66.7 %shard_map.85 = (f32[24,64,128]{2,1,0:T(8,128)}, f32[24,64,128]{2,1,0:T(8,128)}, f32[32,64,128]{2,1,0:T(8,128)}, f32[2,14,32,128]{3,2,1,0:T(8,128)}) custom-call(s32[1,1,24,27]{3,2,1,0:T(8,128)} %kmap_rows.1, s32[1,1,4,8]{3,2,1,0:T(4,128)} %bitcast.3, s32[1,1]{1,0:T(1,128)S(6)} %copy.9.counts, s32[1,1,24,27]{3,2,1,0:T(8,128)} %kmap_rows.1, ...), custom_call_target="tpu_custom_call" | custom-call | tf_op jit(solution)/shard_map/pallas_call | solution.py:440
  68.0 3.8 %shard_map.86 = (f32[24,64,128]{2,1,0:T(8,128)}, f32[24,64,128]{2,1,0:T(8,128)}, f32[27,64,64]{2,1,0:T(8,128)}) custom-call(s32[1,1,4,8]{3,2,1,0:T(4,128)} %bitcast.4, f32[24,64,128]{2,1,0:T(8,128)} %get-tuple-element.10.ge_hbm, f32[32,64,128]{2,1,0:T(8,128)} %get-tuple-element.11.back_hbm, f32[2,14,32,128]{3,2,1,0:T(8,128)} %get-tuple-element.12.summed_hbm, ...), custom_call_target="tpu_custom_call" | custom-call | tf_op jit(solution)/shard_map/pallas_call | solution.py:499
